TPU v7x, 128 devices: a whole 4x4x4 slice. The times are simulated.
128 devices in a mesh: ulysses: 4 (over z_hi, core), blk: 32 (over y, z_lo, x).
Axes of the slice: x: 4, y: 4, z: 4 (z_hi: 2, z_lo: 2; z = z_hi * 2 + z_lo), core: 2. Of those that a mesh axis runs over, the one named last changes fastest.
Arguments:
- query_in: bfloat16 [13312, 2560], P(('ulysses', 'blk')), may hold values from -160 to 160
- key_in: bfloat16 [13312, 2560], P(('ulysses', 'blk')), may hold values from -10 to 10
- value_in: bfloat16 [13312, 2560], P(('ulysses', 'blk')), may hold values from -12 to 12
- residual: bfloat16 [13312, 5120], P(('ulysses', 'blk')), may hold values from -3 to 3
- out_weight: bfloat16 [2560, 5120], P('ulysses'), may hold values from -0.125 to 0.125
- gate_scale: float32 [5120], replicated, may hold values from 0.5 to 1.5
Outputs:
- mixed: bfloat16 [13312, 5120], P(('ulysses', 'blk'))
All inputs are finite; a program needn't handle non-finite values.
Results may differ from a plain program's by a relative error of at most 0.014.
Values may be sent and summed in bfloat16 or wider, within the bound.
No kernel may reach another device: no remote copies, remote signals or barrier semaphores. Data moves between devices by JAX's collectives and lax.ppermute only.
A program may use at most 128 MiB of HBM per device.

v0:
```python
import jax
import jax.numpy as jnp
from jax import lax
from jax.sharding import PartitionSpec as P

HEAD_DIM = 128


def from_behind(x, axis, by):
    devices = lax.axis_size(axis)
    return lax.ppermute(x, axis, [(i, (i + by) % devices) for i in range(devices)])


def absorb(carried, key_part, value_part, query_heads):
    largest, totals, accumulated = carried
    key_heads = key_part.reshape(key_part.shape[0], query_heads.shape[1], HEAD_DIM)
    value_heads = value_part.reshape(value_part.shape[0], query_heads.shape[1], HEAD_DIM)
    scores = jnp.einsum(
        "qhd,khd->qhk", query_heads, key_heads, preferred_element_type=jnp.float32
    ) * HEAD_DIM ** (-0.5)
    new_largest = jnp.maximum(largest, jnp.max(scores, axis=-1))
    correction = jnp.exp(largest - new_largest)
    weights = jnp.exp(scores - new_largest[..., None])
    totals = totals * correction + jnp.sum(weights, axis=-1)
    update = jnp.einsum(
        "qhk,khd->qhd",
        weights.astype(jnp.bfloat16),
        value_heads,
        preferred_element_type=jnp.float32,
    )
    accumulated = accumulated * correction[..., None] + update
    return (new_largest, totals, accumulated)


def on_device(query_in, key_in, value_in, residual, out_weight, gate_scale):
    query_local, keys_local, values_local = (
        lax.all_to_all(query_in, "ulysses", split_axis=1, concat_axis=0, tiled=True),
        lax.all_to_all(key_in, "ulysses", split_axis=1, concat_axis=0, tiled=True),
        lax.all_to_all(value_in, "ulysses", split_axis=1, concat_axis=0, tiled=True),
    )
    row_count = query_local.shape[0]
    local_width = query_local.shape[1]
    heads_here = local_width // HEAD_DIM
    query_heads = query_local.reshape(row_count, heads_here, HEAD_DIM)
    initial = (
        jnp.full((row_count, heads_here), -1e30, jnp.float32),
        jnp.zeros((row_count, heads_here), jnp.float32),
        jnp.zeros((row_count, heads_here, HEAD_DIM), jnp.float32),
    )

    def turn_forward(turn_index, carry):
        carried, key_buffer, value_buffer = carry
        carried = absorb(carried, key_buffer, value_buffer, query_heads)
        key_buffer, value_buffer = from_behind((key_buffer, value_buffer), "blk", 1)
        return (carried, key_buffer, value_buffer)

    carried, key_buffer, value_buffer = lax.fori_loop(
        0, lax.axis_size("blk") - 1, turn_forward, (initial, keys_local, values_local)
    )
    carried = absorb(carried, key_buffer, value_buffer, query_heads)
    largest, totals, accumulated = carried
    attended = (
        (accumulated / totals[..., None]).reshape(row_count, local_width).astype(jnp.bfloat16)
    )
    summed = lax.psum_scatter(
        jnp.dot(attended, out_weight, preferred_element_type=jnp.float32).astype(jnp.bfloat16),
        "ulysses",
        scatter_dimension=0,
        tiled=True,
    ).astype(jnp.float32)
    return (residual.astype(jnp.float32) + gate_scale * summed).astype(jnp.bfloat16)


def solution(mesh):
    return jax.shard_map(
        on_device,
        mesh=mesh,
        in_specs=(
            P(("ulysses", "blk"), None),
            P(("ulysses", "blk"), None),
            P(("ulysses", "blk"), None),
            P(("ulysses", "blk"), None),
            P("ulysses", None),
            P(),
        ),
        out_specs=P(("ulysses", "blk"), None),
        check_vma=False,
    )
```

profile of v0, /device:TPU:1, one launch (start us, length us, event | category | flops | bytes accessed | tf_op | source)
XLA Modules:
  0.0 953.3 jit_solution(11598633297255452609)
XLA Ops:
  54.0 792.2 %while.19 = (s32[]{:T(128)}, f32[416,5]{0,1:T(8,128)S(1)}, f32[416,5]{0,1:T(8,128)S(1)}, f32[416,5,128]{2,0,1:T(8,128)S(1)}, bf16[416,640]{1,0:T(8,128)(2,1)}, /...) while((s32[]{:T(128)}, f32[416,5]{0,1:T(8,128)S(1)}, ...), condition=%wide.region_3.0_spmd.clone, body=%wide.region_0.0_spmd.clone.sunk | while | flops 450754720 | bytes 22763704 | solution.py:57
  72.1 11.4 %collective-permute-done.1 = bf16[416,640]{1,0:T(8,128)(2,1)} collective-permute-done((bf16[416,640]{1,0:T(8,128)(2,1)S(1)}, bf16[416,640]{1,0:T(8,128)(2,1)}, u32[]{:S(2)}, u32[]{:S(2)}) %collective-permute-start.1) | collective-permute-done | bytes 532512 | tf_op jit(solution)/shard_map/while/body/eval_jaxpr/ppermute | solution.py:11
  90.5 10.2 %collective-permute-done = bf16[416,640]{1,0:T(8,128)(2,1)} collective-permute-done((bf16[416,640]{1,0:T(8,128)(2,1)S(1)}, bf16[416,640]{1,0:T(8,128)(2,1)}, u32[]{:S(2)}, u32[]{:S(2)}) %collective-permute-start) | collective-permute-done | bytes 532512 | tf_op jit(solution)/shard_map/while/body/eval_jaxpr/ppermute | solution.py:11
  100.7 11.4 %collective-permute-done.1 = bf16[416,640]{1,0:T(8,128)(2,1)} collective-permute-done((bf16[416,640]{1,0:T(8,128)(2,1)S(1)}, bf16[416,640]{1,0:T(8,128)(2,1)}, u32[]{:S(2)}, u32[]{:S(2)}) %collective-permute-start.1) | collective-permute-done | bytes 532512 | tf_op jit(solution)/shard_map/while/body/eval_jaxpr/ppermute | solution.py:11
  128.4 11.4 %collective-permute-done.1 = bf16[416,640]{1,0:T(8,128)(2,1)} collective-permute-done((bf16[416,640]{1,0:T(8,128)(2,1)S(1)}, bf16[416,640]{1,0:T(8,128)(2,1)}, u32[]{:S(2)}, u32[]{:S(2)}) %collective-permute-start.1) | collective-permute-done | bytes 532512 | tf_op jit(solution)/shard_map/while/body/eval_jaxpr/ppermute | solution.py:11
  155.1 11.4 %collective-permute-done.1 = bf16[416,640]{1,0:T(8,128)(2,1)} collective-permute-done((bf16[416,640]{1,0:T(8,128)(2,1)S(1)}, bf16[416,640]{1,0:T(8,128)(2,1)}, u32[]{:S(2)}, u32[]{:S(2)}) %collective-permute-start.1) | collective-permute-done | bytes 532512 | tf_op jit(solution)/shard_map/while/body/eval_jaxpr/ppermute | solution.py:11
  181.0 11.4 %collective-permute-done.1 = bf16[416,640]{1,0:T(8,128)(2,1)} collective-permute-done((bf16[416,640]{1,0:T(8,128)(2,1)S(1)}, bf16[416,640]{1,0:T(8,128)(2,1)}, u32[]{:S(2)}, u32[]{:S(2)}) %collective-permute-start.1) | collective-permute-done | bytes 532512 | tf_op jit(solution)/shard_map/while/body/eval_jaxpr/ppermute | solution.py:11
  205.9 11.4 %collective-permute-done.1 = bf16[416,640]{1,0:T(8,128)(2,1)} collective-permute-done((bf16[416,640]{1,0:T(8,128)(2,1)S(1)}, bf16[416,640]{1,0:T(8,128)(2,1)}, u32[]{:S(2)}, u32[]{:S(2)}) %collective-permute-start.1) | collective-permute-done | bytes 532512 | tf_op jit(solution)/shard_map/while/body/eval_jaxpr/ppermute | solution.py:11
  230.8 10.5 %collective-permute-done.1 = bf16[416,640]{1,0:T(8,128)(2,1)} collective-permute-done((bf16[416,640]{1,0:T(8,128)(2,1)S(1)}, bf16[416,640]{1,0:T(8,128)(2,1)}, u32[]{:S(2)}, u32[]{:S(2)}) %collective-permute-start.1) | collective-permute-done | bytes 532512 | tf_op jit(solution)/shard_map/while/body/eval_jaxpr/ppermute | solution.py:11
  254.8 9.6 %collective-permute-done.1 = bf16[416,640]{1,0:T(8,128)(2,1)} collective-permute-done((bf16[416,640]{1,0:T(8,128)(2,1)S(1)}, bf16[416,640]{1,0:T(8,128)(2,1)}, u32[]{:S(2)}, u32[]{:S(2)}) %collective-permute-start.1) | collective-permute-done | bytes 532512 | tf_op jit(solution)/shard_map/while/body/eval_jaxpr/ppermute | solution.py:11
  359.4 9.7 %collective-permute-done = bf16[416,640]{1,0:T(8,128)(2,1)} collective-permute-done((bf16[416,640]{1,0:T(8,128)(2,1)S(1)}, bf16[416,640]{1,0:T(8,128)(2,1)}, u32[]{:S(2)}, u32[]{:S(2)}) %collective-permute-start) | collective-permute-done | bytes 532512 | tf_op jit(solution)/shard_map/while/body/eval_jaxpr/ppermute | solution.py:11
  381.8 10.8 %collective-permute-done = bf16[416,640]{1,0:T(8,128)(2,1)} collective-permute-done((bf16[416,640]{1,0:T(8,128)(2,1)S(1)}, bf16[416,640]{1,0:T(8,128)(2,1)}, u32[]{:S(2)}, u32[]{:S(2)}) %collective-permute-start) | collective-permute-done | bytes 532512 | tf_op jit(solution)/shard_map/while/body/eval_jaxpr/ppermute | solution.py:11
  405.4 11.9 %collective-permute-done = bf16[416,640]{1,0:T(8,128)(2,1)} collective-permute-done((bf16[416,640]{1,0:T(8,128)(2,1)S(1)}, bf16[416,640]{1,0:T(8,128)(2,1)}, u32[]{:S(2)}, u32[]{:S(2)}) %collective-permute-start) | collective-permute-done | bytes 532512 | tf_op jit(solution)/shard_map/while/body/eval_jaxpr/ppermute | solution.py:11
  430.0 12.6 %collective-permute-done = bf16[416,640]{1,0:T(8,128)(2,1)} collective-permute-done((bf16[416,640]{1,0:T(8,128)(2,1)S(1)}, bf16[416,640]{1,0:T(8,128)(2,1)}, u32[]{:S(2)}, u32[]{:S(2)}) %collective-permute-start) | collective-permute-done | bytes 532512 | tf_op jit(solution)/shard_map/while/body/eval_jaxpr/ppermute | solution.py:11
  455.6 12.6 %collective-permute-done = bf16[416,640]{1,0:T(8,128)(2,1)} collective-permute-done((bf16[416,640]{1,0:T(8,128)(2,1)S(1)}, bf16[416,640]{1,0:T(8,128)(2,1)}, u32[]{:S(2)}, u32[]{:S(2)}) %collective-permute-start) | collective-permute-done | bytes 532512 | tf_op jit(solution)/shard_map/while/body/eval_jaxpr/ppermute | solution.py:11
  482.4 12.6 %collective-permute-done = bf16[416,640]{1,0:T(8,128)(2,1)} collective-permute-done((bf16[416,640]{1,0:T(8,128)(2,1)S(1)}, bf16[416,640]{1,0:T(8,128)(2,1)}, u32[]{:S(2)}, u32[]{:S(2)}) %collective-permute-start) | collective-permute-done | bytes 532512 | tf_op jit(solution)/shard_map/while/body/eval_jaxpr/ppermute | solution.py:11
  510.2 12.6 %collective-permute-done = bf16[416,640]{1,0:T(8,128)(2,1)} collective-permute-done((bf16[416,640]{1,0:T(8,128)(2,1)S(1)}, bf16[416,640]{1,0:T(8,128)(2,1)}, u32[]{:S(2)}, u32[]{:S(2)}) %collective-permute-start) | collective-permute-done | bytes 532512 | tf_op jit(solution)/shard_map/while/body/eval_jaxpr/ppermute | solution.py:11
  539.1 12.4 %collective-permute-done = bf16[416,640]{1,0:T(8,128)(2,1)} collective-permute-done((bf16[416,640]{1,0:T(8,128)(2,1)S(1)}, bf16[416,640]{1,0:T(8,128)(2,1)}, u32[]{:S(2)}, u32[]{:S(2)}) %collective-permute-start) | collective-permute-done | bytes 532512 | tf_op jit(solution)/shard_map/while/body/eval_jaxpr/ppermute | solution.py:11
  551.6 10.6 %collective-permute-done.1 = bf16[416,640]{1,0:T(8,128)(2,1)} collective-permute-done((bf16[416,640]{1,0:T(8,128)(2,1)S(1)}, bf16[416,640]{1,0:T(8,128)(2,1)}, u32[]{:S(2)}, u32[]{:S(2)}) %collective-permute-start.1) | collective-permute-done | bytes 532512 | tf_op jit(solution)/shard_map/while/body/eval_jaxpr/ppermute | solution.py:11
  569.1 11.9 %collective-permute-done = bf16[416,640]{1,0:T(8,128)(2,1)} collective-permute-done((bf16[416,640]{1,0:T(8,128)(2,1)S(1)}, bf16[416,640]{1,0:T(8,128)(2,1)}, u32[]{:S(2)}, u32[]{:S(2)}) %collective-permute-start) | collective-permute-done | bytes 532512 | tf_op jit(solution)/shard_map/while/body/eval_jaxpr/ppermute | solution.py:11
  581.1 11.4 %collective-permute-done.1 = bf16[416,640]{1,0:T(8,128)(2,1)} collective-permute-done((bf16[416,640]{1,0:T(8,128)(2,1)S(1)}, bf16[416,640]{1,0:T(8,128)(2,1)}, u32[]{:S(2)}, u32[]{:S(2)}) %collective-permute-start.1) | collective-permute-done | bytes 532512 | tf_op jit(solution)/shard_map/while/body/eval_jaxpr/ppermute | solution.py:11
  599.5 11.0 %collective-permute-done = bf16[416,640]{1,0:T(8,128)(2,1)} collective-permute-done((bf16[416,640]{1,0:T(8,128)(2,1)S(1)}, bf16[416,640]{1,0:T(8,128)(2,1)}, u32[]{:S(2)}, u32[]{:S(2)}) %collective-permute-start) | collective-permute-done | bytes 532512 | tf_op jit(solution)/shard_map/while/body/eval_jaxpr/ppermute | solution.py:11
  610.5 11.4 %collective-permute-done.1 = bf16[416,640]{1,0:T(8,128)(2,1)} collective-permute-done((bf16[416,640]{1,0:T(8,128)(2,1)S(1)}, bf16[416,640]{1,0:T(8,128)(2,1)}, u32[]{:S(2)}, u32[]{:S(2)}) %collective-permute-start.1) | collective-permute-done | bytes 532512 | tf_op jit(solution)/shard_map/while/body/eval_jaxpr/ppermute | solution.py:11
  628.9 10.1 %collective-permute-done = bf16[416,640]{1,0:T(8,128)(2,1)} collective-permute-done((bf16[416,640]{1,0:T(8,128)(2,1)S(1)}, bf16[416,640]{1,0:T(8,128)(2,1)}, u32[]{:S(2)}, u32[]{:S(2)}) %collective-permute-start) | collective-permute-done | bytes 532512 | tf_op jit(solution)/shard_map/while/body/eval_jaxpr/ppermute | solution.py:11
  639.0 11.4 %collective-permute-done.1 = bf16[416,640]{1,0:T(8,128)(2,1)} collective-permute-done((bf16[416,640]{1,0:T(8,128)(2,1)S(1)}, bf16[416,640]{1,0:T(8,128)(2,1)}, u32[]{:S(2)}, u32[]{:S(2)}) %collective-permute-start.1) | collective-permute-done | bytes 532512 | tf_op jit(solution)/shard_map/while/body/eval_jaxpr/ppermute | solution.py:11
  666.6 11.4 %collective-permute-done.1 = bf16[416,640]{1,0:T(8,128)(2,1)} collective-permute-done((bf16[416,640]{1,0:T(8,128)(2,1)S(1)}, bf16[416,640]{1,0:T(8,128)(2,1)}, u32[]{:S(2)}, u32[]{:S(2)}) %collective-permute-start.1) | collective-permute-done | bytes 532512 | tf_op jit(solution)/shard_map/while/body/eval_jaxpr/ppermute | solution.py:11
  693.3 11.4 %collective-permute-done.1 = bf16[416,640]{1,0:T(8,128)(2,1)} collective-permute-done((bf16[416,640]{1,0:T(8,128)(2,1)S(1)}, bf16[416,640]{1,0:T(8,128)(2,1)}, u32[]{:S(2)}, u32[]{:S(2)}) %collective-permute-start.1) | collective-permute-done | bytes 532512 | tf_op jit(solution)/shard_map/while/body/eval_jaxpr/ppermute | solution.py:11
  719.0 11.4 %collective-permute-done.1 = bf16[416,640]{1,0:T(8,128)(2,1)} collective-permute-done((bf16[416,640]{1,0:T(8,128)(2,1)S(1)}, bf16[416,640]{1,0:T(8,128)(2,1)}, u32[]{:S(2)}, u32[]{:S(2)}) %collective-permute-start.1) | collective-permute-done | bytes 532512 | tf_op jit(solution)/shard_map/while/body/eval_jaxpr/ppermute | solution.py:11
  743.9 11.3 %collective-permute-done.1 = bf16[416,640]{1,0:T(8,128)(2,1)} collective-permute-done((bf16[416,640]{1,0:T(8,128)(2,1)S(1)}, bf16[416,640]{1,0:T(8,128)(2,1)}, u32[]{:S(2)}, u32[]{:S(2)}) %collective-permute-start.1) | collective-permute-done | bytes 532512 | tf_op jit(solution)/shard_map/while/body/eval_jaxpr/ppermute | solution.py:11
  768.7 10.4 %collective-permute-done.1 = bf16[416,640]{1,0:T(8,128)(2,1)} collective-permute-done((bf16[416,640]{1,0:T(8,128)(2,1)S(1)}, bf16[416,640]{1,0:T(8,128)(2,1)}, u32[]{:S(2)}, u32[]{:S(2)}) %collective-permute-start.1) | collective-permute-done | bytes 532512 | tf_op jit(solution)/shard_map/while/body/eval_jaxpr/ppermute | solution.py:11
  792.6 9.5 collective-permute-done.1
  861.6 82.3 %reduce-scatter.2.cloned.1.call-done = bf16[104,5120]{1,0:T(8,128)(2,1)} async-done(((bf16[416,5120]{1,0:T(8,128)(2,1)}), bf16[104,5120]{1,0:T(8,128)(2,1)}) %reduce-scatter.2.cloned.1.call-update) | async-done | bytes 1064976 | tf_op jit(solution)/shard_map/reduce_scatter | solution.py:65
  (439 shorter events, 518.5 us)
Async XLA Ops:
  44.3 899.6 %reduce-scatter.2.cloned.1.call-start = ((), (), s32[]{:S(2)}) async-start(), calls=%async_computation.4 | async-start | bytes 5324800 | tf_op jit(solution)/shard_map/reduce_scatter | solution.py:65
  57.3 26.2 %collective-permute-start.1 = (bf16[416,640]{1,0:T(8,128)(2,1)S(1)}, bf16[416,640]{1,0:T(8,128)(2,1)}, u32[]{:S(2)}, u32[]{:S(2)}) collective-permute-start(bf16[416,640]{1,0:T(8,128)(2,1)S(1)} %copy.117), channel_id=1, source_target_pairs={{0,1},{1,2},{2,3},{3,4},{4,5},{5,6},{6,7},{7,8},{8,9},{9,10},{10,1... | collective-permute-start | bytes 1597448 | tf_op jit(solution)/shard_map/while/body/eval_jaxpr/ppermute | solution.py:11
  85.6 26.5 %collective-permute-start.1 = (bf16[416,640]{1,0:T(8,128)(2,1)S(1)}, bf16[416,640]{1,0:T(8,128)(2,1)}, u32[]{:S(2)}, u32[]{:S(2)}) collective-permute-start(bf16[416,640]{1,0:T(8,128)(2,1)S(1)} %copy.117), channel_id=1, source_target_pairs={{0,1},{1,2},{2,3},{3,4},{4,5},{5,6},{6,7},{7,8},{8,9},{9,10},{10,1... | collective-permute-start | bytes 1597448 | tf_op jit(solution)/shard_map/while/body/eval_jaxpr/ppermute | solution.py:11
  114.2 25.6 %collective-permute-start.1 = (bf16[416,640]{1,0:T(8,128)(2,1)S(1)}, bf16[416,640]{1,0:T(8,128)(2,1)}, u32[]{:S(2)}, u32[]{:S(2)}) collective-permute-start(bf16[416,640]{1,0:T(8,128)(2,1)S(1)} %copy.117), channel_id=1, source_target_pairs={{0,1},{1,2},{2,3},{3,4},{4,5},{5,6},{6,7},{7,8},{8,9},{9,10},{10,1... | collective-permute-start | bytes 1597448 | tf_op jit(solution)/shard_map/while/body/eval_jaxpr/ppermute | solution.py:11
  141.9 24.7 %collective-permute-start.1 = (bf16[416,640]{1,0:T(8,128)(2,1)S(1)}, bf16[416,640]{1,0:T(8,128)(2,1)}, u32[]{:S(2)}, u32[]{:S(2)}) collective-permute-start(bf16[416,640]{1,0:T(8,128)(2,1)S(1)} %copy.117), channel_id=1, source_target_pairs={{0,1},{1,2},{2,3},{3,4},{4,5},{5,6},{6,7},{7,8},{8,9},{9,10},{10,1... | collective-permute-start | bytes 1597448 | tf_op jit(solution)/shard_map/while/body/eval_jaxpr/ppermute | solution.py:11
  168.6 23.7 %collective-permute-start.1 = (bf16[416,640]{1,0:T(8,128)(2,1)S(1)}, bf16[416,640]{1,0:T(8,128)(2,1)}, u32[]{:S(2)}, u32[]{:S(2)}) collective-permute-start(bf16[416,640]{1,0:T(8,128)(2,1)S(1)} %copy.117), channel_id=1, source_target_pairs={{0,1},{1,2},{2,3},{3,4},{4,5},{5,6},{6,7},{7,8},{8,9},{9,10},{10,1... | collective-permute-start | bytes 1597448 | tf_op jit(solution)/shard_map/while/body/eval_jaxpr/ppermute | solution.py:11
  194.5 22.8 %collective-permute-start.1 = (bf16[416,640]{1,0:T(8,128)(2,1)S(1)}, bf16[416,640]{1,0:T(8,128)(2,1)}, u32[]{:S(2)}, u32[]{:S(2)}) collective-permute-start(bf16[416,640]{1,0:T(8,128)(2,1)S(1)} %copy.117), channel_id=1, source_target_pairs={{0,1},{1,2},{2,3},{3,4},{4,5},{5,6},{6,7},{7,8},{8,9},{9,10},{10,1... | collective-permute-start | bytes 1597448 | tf_op jit(solution)/shard_map/while/body/eval_jaxpr/ppermute | solution.py:11
  219.4 21.9 %collective-permute-start.1 = (bf16[416,640]{1,0:T(8,128)(2,1)S(1)}, bf16[416,640]{1,0:T(8,128)(2,1)}, u32[]{:S(2)}, u32[]{:S(2)}) collective-permute-start(bf16[416,640]{1,0:T(8,128)(2,1)S(1)} %copy.117), channel_id=1, source_target_pairs={{0,1},{1,2},{2,3},{3,4},{4,5},{5,6},{6,7},{7,8},{8,9},{9,10},{10,1... | collective-permute-start | bytes 1597448 | tf_op jit(solution)/shard_map/while/body/eval_jaxpr/ppermute | solution.py:11
  243.4 21.0 %collective-permute-start.1 = (bf16[416,640]{1,0:T(8,128)(2,1)S(1)}, bf16[416,640]{1,0:T(8,128)(2,1)}, u32[]{:S(2)}, u32[]{:S(2)}) collective-permute-start(bf16[416,640]{1,0:T(8,128)(2,1)S(1)} %copy.117), channel_id=1, source_target_pairs={{0,1},{1,2},{2,3},{3,4},{4,5},{5,6},{6,7},{7,8},{8,9},{9,10},{10,1... | collective-permute-start | bytes 1597448 | tf_op jit(solution)/shard_map/while/body/eval_jaxpr/ppermute | solution.py:11
  266.5 20.1 %collective-permute-start.1 = (bf16[416,640]{1,0:T(8,128)(2,1)S(1)}, bf16[416,640]{1,0:T(8,128)(2,1)}, u32[]{:S(2)}, u32[]{:S(2)}) collective-permute-start(bf16[416,640]{1,0:T(8,128)(2,1)S(1)} %copy.117), channel_id=1, source_target_pairs={{0,1},{1,2},{2,3},{3,4},{4,5},{5,6},{6,7},{7,8},{8,9},{9,10},{10,1... | collective-permute-start | bytes 1597448 | tf_op jit(solution)/shard_map/while/body/eval_jaxpr/ppermute | solution.py:11
  288.6 19.9 %collective-permute-start.1 = (bf16[416,640]{1,0:T(8,128)(2,1)S(1)}, bf16[416,640]{1,0:T(8,128)(2,1)}, u32[]{:S(2)}, u32[]{:S(2)}) collective-permute-start(bf16[416,640]{1,0:T(8,128)(2,1)S(1)} %copy.117), channel_id=1, source_target_pairs={{0,1},{1,2},{2,3},{3,4},{4,5},{5,6},{6,7},{7,8},{8,9},{9,10},{10,1... | collective-permute-start | bytes 1597448 | tf_op jit(solution)/shard_map/while/body/eval_jaxpr/ppermute | solution.py:11
  310.6 19.9 %collective-permute-start.1 = (bf16[416,640]{1,0:T(8,128)(2,1)S(1)}, bf16[416,640]{1,0:T(8,128)(2,1)}, u32[]{:S(2)}, u32[]{:S(2)}) collective-permute-start(bf16[416,640]{1,0:T(8,128)(2,1)S(1)} %copy.117), channel_id=1, source_target_pairs={{0,1},{1,2},{2,3},{3,4},{4,5},{5,6},{6,7},{7,8},{8,9},{9,10},{10,1... | collective-permute-start | bytes 1597448 | tf_op jit(solution)/shard_map/while/body/eval_jaxpr/ppermute | solution.py:11
  332.5 19.9 %collective-permute-start.1 = (bf16[416,640]{1,0:T(8,128)(2,1)S(1)}, bf16[416,640]{1,0:T(8,128)(2,1)}, u32[]{:S(2)}, u32[]{:S(2)}) collective-permute-start(bf16[416,640]{1,0:T(8,128)(2,1)S(1)} %copy.117), channel_id=1, source_target_pairs={{0,1},{1,2},{2,3},{3,4},{4,5},{5,6},{6,7},{7,8},{8,9},{9,10},{10,1... | collective-permute-start | bytes 1597448 | tf_op jit(solution)/shard_map/while/body/eval_jaxpr/ppermute | solution.py:11
  354.5 20.3 %collective-permute-start.1 = (bf16[416,640]{1,0:T(8,128)(2,1)S(1)}, bf16[416,640]{1,0:T(8,128)(2,1)}, u32[]{:S(2)}, u32[]{:S(2)}) collective-permute-start(bf16[416,640]{1,0:T(8,128)(2,1)S(1)} %copy.117), channel_id=1, source_target_pairs={{0,1},{1,2},{2,3},{3,4},{4,5},{5,6},{6,7},{7,8},{8,9},{9,10},{10,1... | collective-permute-start | bytes 1597448 | tf_op jit(solution)/shard_map/while/body/eval_jaxpr/ppermute | solution.py:11
  376.9 21.4 %collective-permute-start.1 = (bf16[416,640]{1,0:T(8,128)(2,1)S(1)}, bf16[416,640]{1,0:T(8,128)(2,1)}, u32[]{:S(2)}, u32[]{:S(2)}) collective-permute-start(bf16[416,640]{1,0:T(8,128)(2,1)S(1)} %copy.117), channel_id=1, source_target_pairs={{0,1},{1,2},{2,3},{3,4},{4,5},{5,6},{6,7},{7,8},{8,9},{9,10},{10,1... | collective-permute-start | bytes 1597448 | tf_op jit(solution)/shard_map/while/body/eval_jaxpr/ppermute | solution.py:11
  400.5 22.5 %collective-permute-start.1 = (bf16[416,640]{1,0:T(8,128)(2,1)S(1)}, bf16[416,640]{1,0:T(8,128)(2,1)}, u32[]{:S(2)}, u32[]{:S(2)}) collective-permute-start(bf16[416,640]{1,0:T(8,128)(2,1)S(1)} %copy.117), channel_id=1, source_target_pairs={{0,1},{1,2},{2,3},{3,4},{4,5},{5,6},{6,7},{7,8},{8,9},{9,10},{10,1... | collective-permute-start | bytes 1597448 | tf_op jit(solution)/shard_map/while/body/eval_jaxpr/ppermute | solution.py:11
  425.1 23.6 %collective-permute-start.1 = (bf16[416,640]{1,0:T(8,128)(2,1)S(1)}, bf16[416,640]{1,0:T(8,128)(2,1)}, u32[]{:S(2)}, u32[]{:S(2)}) collective-permute-start(bf16[416,640]{1,0:T(8,128)(2,1)S(1)} %copy.117), channel_id=1, source_target_pairs={{0,1},{1,2},{2,3},{3,4},{4,5},{5,6},{6,7},{7,8},{8,9},{9,10},{10,1... | collective-permute-start | bytes 1597448 | tf_op jit(solution)/shard_map/while/body/eval_jaxpr/ppermute | solution.py:11
  450.7 24.7 %collective-permute-start.1 = (bf16[416,640]{1,0:T(8,128)(2,1)S(1)}, bf16[416,640]{1,0:T(8,128)(2,1)}, u32[]{:S(2)}, u32[]{:S(2)}) collective-permute-start(bf16[416,640]{1,0:T(8,128)(2,1)S(1)} %copy.117), channel_id=1, source_target_pairs={{0,1},{1,2},{2,3},{3,4},{4,5},{5,6},{6,7},{7,8},{8,9},{9,10},{10,1... | collective-permute-start | bytes 1597448 | tf_op jit(solution)/shard_map/while/body/eval_jaxpr/ppermute | solution.py:11
  477.5 25.7 %collective-permute-start.1 = (bf16[416,640]{1,0:T(8,128)(2,1)S(1)}, bf16[416,640]{1,0:T(8,128)(2,1)}, u32[]{:S(2)}, u32[]{:S(2)}) collective-permute-start(bf16[416,640]{1,0:T(8,128)(2,1)S(1)} %copy.117), channel_id=1, source_target_pairs={{0,1},{1,2},{2,3},{3,4},{4,5},{5,6},{6,7},{7,8},{8,9},{9,10},{10,1... | collective-permute-start | bytes 1597448 | tf_op jit(solution)/shard_map/while/body/eval_jaxpr/ppermute | solution.py:11
  505.3 26.8 %collective-permute-start.1 = (bf16[416,640]{1,0:T(8,128)(2,1)S(1)}, bf16[416,640]{1,0:T(8,128)(2,1)}, u32[]{:S(2)}, u32[]{:S(2)}) collective-permute-start(bf16[416,640]{1,0:T(8,128)(2,1)S(1)} %copy.117), channel_id=1, source_target_pairs={{0,1},{1,2},{2,3},{3,4},{4,5},{5,6},{6,7},{7,8},{8,9},{9,10},{10,1... | collective-permute-start | bytes 1597448 | tf_op jit(solution)/shard_map/while/body/eval_jaxpr/ppermute | solution.py:11
  534.2 27.9 %collective-permute-start.1 = (bf16[416,640]{1,0:T(8,128)(2,1)S(1)}, bf16[416,640]{1,0:T(8,128)(2,1)}, u32[]{:S(2)}, u32[]{:S(2)}) collective-permute-start(bf16[416,640]{1,0:T(8,128)(2,1)S(1)} %copy.117), channel_id=1, source_target_pairs={{0,1},{1,2},{2,3},{3,4},{4,5},{5,6},{6,7},{7,8},{8,9},{9,10},{10,1... | collective-permute-start | bytes 1597448 | tf_op jit(solution)/shard_map/while/body/eval_jaxpr/ppermute | solution.py:11
  564.2 28.2 %collective-permute-start.1 = (bf16[416,640]{1,0:T(8,128)(2,1)S(1)}, bf16[416,640]{1,0:T(8,128)(2,1)}, u32[]{:S(2)}, u32[]{:S(2)}) collective-permute-start(bf16[416,640]{1,0:T(8,128)(2,1)S(1)} %copy.117), channel_id=1, source_target_pairs={{0,1},{1,2},{2,3},{3,4},{4,5},{5,6},{6,7},{7,8},{8,9},{9,10},{10,1... | collective-permute-start | bytes 1597448 | tf_op jit(solution)/shard_map/while/body/eval_jaxpr/ppermute | solution.py:11
  594.6 27.3 %collective-permute-start.1 = (bf16[416,640]{1,0:T(8,128)(2,1)S(1)}, bf16[416,640]{1,0:T(8,128)(2,1)}, u32[]{:S(2)}, u32[]{:S(2)}) collective-permute-start(bf16[416,640]{1,0:T(8,128)(2,1)S(1)} %copy.117), channel_id=1, source_target_pairs={{0,1},{1,2},{2,3},{3,4},{4,5},{5,6},{6,7},{7,8},{8,9},{9,10},{10,1... | collective-permute-start | bytes 1597448 | tf_op jit(solution)/shard_map/while/body/eval_jaxpr/ppermute | solution.py:11
  624.0 26.4 %collective-permute-start.1 = (bf16[416,640]{1,0:T(8,128)(2,1)S(1)}, bf16[416,640]{1,0:T(8,128)(2,1)}, u32[]{:S(2)}, u32[]{:S(2)}) collective-permute-start(bf16[416,640]{1,0:T(8,128)(2,1)S(1)} %copy.117), channel_id=1, source_target_pairs={{0,1},{1,2},{2,3},{3,4},{4,5},{5,6},{6,7},{7,8},{8,9},{9,10},{10,1... | collective-permute-start | bytes 1597448 | tf_op jit(solution)/shard_map/while/body/eval_jaxpr/ppermute | solution.py:11
  652.5 25.5 %collective-permute-start.1 = (bf16[416,640]{1,0:T(8,128)(2,1)S(1)}, bf16[416,640]{1,0:T(8,128)(2,1)}, u32[]{:S(2)}, u32[]{:S(2)}) collective-permute-start(bf16[416,640]{1,0:T(8,128)(2,1)S(1)} %copy.117), channel_id=1, source_target_pairs={{0,1},{1,2},{2,3},{3,4},{4,5},{5,6},{6,7},{7,8},{8,9},{9,10},{10,1... | collective-permute-start | bytes 1597448 | tf_op jit(solution)/shard_map/while/body/eval_jaxpr/ppermute | solution.py:11
  680.1 24.6 %collective-permute-start.1 = (bf16[416,640]{1,0:T(8,128)(2,1)S(1)}, bf16[416,640]{1,0:T(8,128)(2,1)}, u32[]{:S(2)}, u32[]{:S(2)}) collective-permute-start(bf16[416,640]{1,0:T(8,128)(2,1)S(1)} %copy.117), channel_id=1, source_target_pairs={{0,1},{1,2},{2,3},{3,4},{4,5},{5,6},{6,7},{7,8},{8,9},{9,10},{10,1... | collective-permute-start | bytes 1597448 | tf_op jit(solution)/shard_map/while/body/eval_jaxpr/ppermute | solution.py:11
  706.8 23.6 %collective-permute-start.1 = (bf16[416,640]{1,0:T(8,128)(2,1)S(1)}, bf16[416,640]{1,0:T(8,128)(2,1)}, u32[]{:S(2)}, u32[]{:S(2)}) collective-permute-start(bf16[416,640]{1,0:T(8,128)(2,1)S(1)} %copy.117), channel_id=1, source_target_pairs={{0,1},{1,2},{2,3},{3,4},{4,5},{5,6},{6,7},{7,8},{8,9},{9,10},{10,1... | collective-permute-start | bytes 1597448 | tf_op jit(solution)/shard_map/while/body/eval_jaxpr/ppermute | solution.py:11
  732.5 22.7 %collective-permute-start.1 = (bf16[416,640]{1,0:T(8,128)(2,1)S(1)}, bf16[416,640]{1,0:T(8,128)(2,1)}, u32[]{:S(2)}, u32[]{:S(2)}) collective-permute-start(bf16[416,640]{1,0:T(8,128)(2,1)S(1)} %copy.117), channel_id=1, source_target_pairs={{0,1},{1,2},{2,3},{3,4},{4,5},{5,6},{6,7},{7,8},{8,9},{9,10},{10,1... | collective-permute-start | bytes 1597448 | tf_op jit(solution)/shard_map/while/body/eval_jaxpr/ppermute | solution.py:11
  757.3 21.8 %collective-permute-start.1 = (bf16[416,640]{1,0:T(8,128)(2,1)S(1)}, bf16[416,640]{1,0:T(8,128)(2,1)}, u32[]{:S(2)}, u32[]{:S(2)}) collective-permute-start(bf16[416,640]{1,0:T(8,128)(2,1)S(1)} %copy.117), channel_id=1, source_target_pairs={{0,1},{1,2},{2,3},{3,4},{4,5},{5,6},{6,7},{7,8},{8,9},{9,10},{10,1... | collective-permute-start | bytes 1597448 | tf_op jit(solution)/shard_map/while/body/eval_jaxpr/ppermute | solution.py:11
  781.2 20.9 %collective-permute-start.1 = (bf16[416,640]{1,0:T(8,128)(2,1)S(1)}, bf16[416,640]{1,0:T(8,128)(2,1)}, u32[]{:S(2)}, u32[]{:S(2)}) collective-permute-start(bf16[416,640]{1,0:T(8,128)(2,1)S(1)} %copy.117), channel_id=1, source_target_pairs={{0,1},{1,2},{2,3},{3,4},{4,5},{5,6},{6,7},{7,8},{8,9},{9,10},{10,1... | collective-permute-start | bytes 1597448 | tf_op jit(solution)/shard_map/while/body/eval_jaxpr/ppermute | solution.py:11
  804.2 20.0 %collective-permute-start.1 = (bf16[416,640]{1,0:T(8,128)(2,1)S(1)}, bf16[416,640]{1,0:T(8,128)(2,1)}, u32[]{:S(2)}, u32[]{:S(2)}) collective-permute-start(bf16[416,640]{1,0:T(8,128)(2,1)S(1)} %copy.117), channel_id=1, source_target_pairs={{0,1},{1,2},{2,3},{3,4},{4,5},{5,6},{6,7},{7,8},{8,9},{9,10},{10,1... | collective-permute-start | bytes 1597448 | tf_op jit(solution)/shard_map/while/body/eval_jaxpr/ppermute | solution.py:11
  826.3 19.9 %collective-permute-start.1 = (bf16[416,640]{1,0:T(8,128)(2,1)S(1)}, bf16[416,640]{1,0:T(8,128)(2,1)}, u32[]{:S(2)}, u32[]{:S(2)}) collective-permute-start(bf16[416,640]{1,0:T(8,128)(2,1)S(1)} %copy.117), channel_id=1, source_target_pairs={{0,1},{1,2},{2,3},{3,4},{4,5},{5,6},{6,7},{7,8},{8,9},{9,10},{10,1... | collective-permute-start | bytes 1597448 | tf_op jit(solution)/shard_map/while/body/eval_jaxpr/ppermute | solution.py:11
  (38 other events, 708.7 us)
Sparse Core Ops, SparseCore 0:
  861.7 82.1 reduce-scatter.1
where the time goes:
time: 958 us; the launch traced here: 953 us
  waiting for transfers between devices  679 us (71%)
  matrix products  122 us (13%)
  local copies, waits for them, and re-layouts  90.2 us (9%)
  other arithmetic  27 us (3%)
  starting transfers between devices  19.2 us (2%)
  between operations  13.5 us (1%)
    ppermute x62, waiting for transfers between devices, from_behind(): lax.ppermute(x, axis, [(i, (i + by) % devices) for i in range(devices)])  573 us
    reduce_scatter x1, waiting for transfers between devices, on_device(): lax.psum_scatter(jnp.dot(attended, out_weight, preferred_element_type=jnp...  82.3 us
    while x155, local copies, waits for them, and re-layouts  80.5 us
    dot_general x32, matrix products, absorb(): jnp.einsum('qhd,khd->qhk', query_heads, key_heads, preferred_element_type...  59.2 us
    dot_general x32, matrix products, absorb(): jnp.einsum('qhk,khd->qhd', weights.astype(jnp.bfloat16), value_heads, pre...  54.9 us
    reduce_sum x32, other arithmetic, absorb(): totals = totals * correction + jnp.sum(weights, axis=-1)  23.8 us
  transfers between devices with their start and end apart: 66, of which 66 were waited for; matrix products, arithmetic and copies ran while one was open for 20% of the time, Pallas kernels for 0%

commit v1 on v0

v1 whole, which is shorter than its diff:
```python
import functools

import jax
import jax.numpy as jnp
from jax import lax
from jax.experimental import pallas as pl
from jax.experimental.pallas import tpu as pltpu
from jax.sharding import Mesh
from jax.sharding import PartitionSpec as P

HEAD_DIM = 128
LANES = 128
SCALE = HEAD_DIM**-0.5 * 1.4426950408889634
ALL = ("zh", "c", "y", "zl", "x")
SIZES = {"zh": 2, "c": 2, "y": 4, "zl": 2, "x": 4}
Z = ("zh", "zl")
CZ = ("c", "zh", "zl")
KEY_TILE = 256
LEVEL_ROWS = 16
F32 = jnp.float32
BF16 = jnp.bfloat16
NT = (((1,), (1,)), ((), ()))


def move(x, place):
    pairs = []
    for at in range(128):
        left, coords = at, {}
        for name in reversed(ALL):
            left, coords[name] = divmod(left, SIZES[name])
        target = place(dict(coords))
        to = 0
        for name in ALL:
            to = to * SIZES[name] + target[name] % SIZES[name]
        pairs.append((at, to))
    return lax.ppermute(x, ALL, pairs)


def along(x, by, keys):
    def place(at):
        at["y" if (at["c"] == 0) == keys else "x"] += by
        return at

    return move(x, place)


def flip(x, *names):
    return move(x, lambda at: {n: 1 - v if n in names else v for n, v in at.items()})


def cut_body(q, k, v, shared, first, second):
    for i, x in enumerate((q, k, v)):
        for z in range(4):
            for out, heads in ((shared, (4,)), (first, (0, 2)), (second, (1, 3))):
                for c, head in enumerate(heads):
                    lanes = slice((5 * z + head) * LANES, (5 * z + head + 1) * LANES)
                    out[4 * c + z, i] = x[:, lanes]


def cut(q, k, v):
    rows = q.shape[0]
    return pl.pallas_call(
        cut_body,
        out_shape=[jax.ShapeDtypeStruct((n, 3, rows, LANES), BF16) for n in (4, 8, 8)],
    )(q, k, v)


def eye(rows):
    return lax.broadcasted_iota(jnp.int32, (rows, LANES), 0) == lax.broadcasted_iota(
        jnp.int32, (rows, LANES), 1
    )


def write_levels(out, at, level):
    rows = level.shape[0]
    lines = []
    for start in range(0, rows, LANES):
        piece = level[start : start + LANES]
        lines.append(jnp.sum(jnp.where(eye(piece.shape[0]), piece, 0.0), axis=0, keepdims=True))
    line = jnp.concatenate(lines, axis=0)
    high = line.astype(BF16).astype(F32)
    middle = (line - high).astype(BF16).astype(F32)
    low = line - high - middle
    spare = jnp.zeros((LEVEL_ROWS - 3 * len(lines), LANES), F32)
    out[at, rows:, :] = jnp.concatenate([high, middle, low, spare], axis=0).astype(BF16)


def read_levels(block, rows):
    n = -(-rows // LANES)
    parts = block[rows:, :].astype(F32)
    return parts[:n] + parts[n : 2 * n] + parts[2 * n : 3 * n]


def column(line, rows):
    pieces = []
    for i, start in enumerate(range(0, rows, LANES)):
        here = min(LANES, rows - start)
        wide = jnp.broadcast_to(line[i : i + 1], (here, LANES))
        pieces.append(jnp.sum(jnp.where(eye(here), wide, 0.0), axis=1, keepdims=True))
    return jnp.concatenate(pieces, axis=0)


def flash_body(n_units, rows, key_rows, *refs):
    q_refs, kv_refs = refs[:n_units], refs[n_units : n_units + 4]
    out, queries, keys, values = refs[n_units + 4 :]
    values[:, HEAD_DIM:] = jnp.ones((4 * key_rows, LANES), BF16)
    for i in range(4):
        part = pl.ds(i * key_rows, key_rows)
        keys[part, :] = kv_refs[i][0]
        values[part, :HEAD_DIM] = kv_refs[i][1]
    for i in range(n_units):
        queries[pl.ds(2 * i * rows, 2 * rows), :] = q_refs[i][...]

    def block(i, _):
        q = queries[pl.ds(pl.multiple_of(i * rows, rows), rows), :]
        largest = total = None
        for start in range(0, 4 * key_rows, KEY_TILE):
            part = pl.ds(start, min(KEY_TILE, 4 * key_rows - start))
            scores = lax.dot_general(q, keys[part, :], NT, preferred_element_type=F32)
            new = jnp.max(scores, axis=1, keepdims=True)
            if total is not None:
                new = jnp.maximum(largest, new)
            weights = jnp.exp2((scores - new) * SCALE).astype(BF16)
            update = jnp.dot(weights, values[part, :], preferred_element_type=F32)
            if total is None:
                total = update
            else:
                total = total * jnp.exp2((largest - new) * SCALE) + update
            largest = new
        sums = total[:, HEAD_DIM:]
        out[i, :rows, :] = (total[:, :HEAD_DIM] / sums).astype(BF16)
        write_levels(out, i, largest * SCALE + jnp.log2(sums))
        return 0

    lax.fori_loop(0, 2 * n_units, block, 0)


def flash(queries, kvs):
    n, rows, key_rows = len(queries), queries[0].shape[0] // 2, kvs[0].shape[1]
    pairs = 2 * n * rows * 4 * key_rows
    out = pl.pallas_call(
        functools.partial(flash_body, n, rows, key_rows),
        out_shape=jax.ShapeDtypeStruct((2 * n, rows + LEVEL_ROWS, LANES), BF16),
        scratch_shapes=[
            pltpu.VMEM((2 * n * rows, HEAD_DIM), BF16),
            pltpu.VMEM((4 * key_rows, HEAD_DIM), BF16),
            pltpu.VMEM((4 * key_rows, 2 * HEAD_DIM), BF16),
        ],
        compiler_params=pltpu.CompilerParams(vmem_limit_bytes=40 << 20),
        cost_estimate=pl.CostEstimate(
            flops=8 * pairs * HEAD_DIM, bytes_accessed=8 * rows * 256 * n, transcendentals=pairs
        ),
    )(*queries, *kvs)
    return [out[2 * i : 2 * i + 2] for i in range(n)]


def merge_blocks(blocks, rows):
    levels = [read_levels(b, rows) for b in blocks]
    top = functools.reduce(jnp.maximum, levels)
    shares = [jnp.exp2(v - top) for v in levels]
    whole = functools.reduce(jnp.add, shares)
    total = 0.0
    for share, b in zip(shares, blocks):
        total = total + column(share / whole, rows) * b[:rows, :].astype(F32)
    return total.astype(BF16), column(top + jnp.log2(whole), rows)


def merge_shared_body(rows, a, b, c, d, mine, other):
    for i, out in enumerate((mine, other)):
        value, level = merge_blocks([x[i] for x in (a, b, c, d)], rows)
        out[0, :rows, :] = value
        write_levels(out, 0, jnp.broadcast_to(level, (rows, LANES)))


def merge_body(rows, a, b, c, d, *rest):
    out = rest[-1] if len(rest) == 1 else rest[2]
    for i in range(2):
        out[i * rows : (i + 1) * rows, :] = merge_blocks([x[i] for x in (a, b, c, d)], rows)[0]
    if len(rest) > 1:
        rest[3][...] = merge_blocks([rest[0][0], rest[1][0]], rows)[0]


def on_device(query_in, key_in, value_in, residual, out_weight, gate_scale):
    own_rows = query_in.shape[0]
    rows = 4 * own_rows
    other_weight = flip(out_weight, "c")
    zh, zl, core = lax.axis_index("zh"), lax.axis_index("zl"), lax.axis_index("c")

    shared, first, second = cut(query_in, key_in, value_in)

    def spread(x, axes):
        got = lax.all_to_all(x, axes, split_axis=0, concat_axis=0, tiled=True)
        return got.transpose(1, 0, 2, 3).reshape(3, got.shape[0] * own_rows, LANES)

    def gather(q, kv):
        return (
            [q, along(q, 1, False), along(q, -1, False), along(q, 2, False)],
            [kv, along(kv, 1, True), along(kv, -1, True), along(kv, 2, True)],
        )

    def send_back(parts):
        return [
            parts[0],
            along(parts[1], -1, False),
            along(parts[2], 1, False),
            along(parts[3], 2, False),
        ]

    got = spread(shared, Z)
    first, got = lax.optimization_barrier((first, got))
    q = jnp.concatenate([got[0], flip(got[0], "c")], axis=0)
    parts = send_back(flash(*gather(q, got[1:])))
    block = jax.ShapeDtypeStruct((1, rows + LEVEL_ROWS, LANES), BF16)
    mine, other = pl.pallas_call(
        functools.partial(merge_shared_body, rows), out_shape=[block, block]
    )(*parts)
    other = flip(other, "c")

    got = spread(first, CZ)
    second, got = lax.optimization_barrier((second, got))
    parts = send_back(flash(*gather(got[0], got[1:])))
    whole = jax.ShapeDtypeStruct((2 * rows, LANES), BF16)
    half = jax.ShapeDtypeStruct((rows, LANES), BF16)
    out_first, out_shared = pl.pallas_call(
        functools.partial(merge_body, rows), out_shape=[whole, half]
    )(*parts, mine, other)

    got = spread(second, CZ)
    queries, kvs = gather(got[0], got[1:])
    away = flash(queries[1:], kvs)
    here = flash(queries[:1], kvs)
    parts = send_back(here + away)
    out_second = pl.pallas_call(functools.partial(merge_body, rows), out_shape=whole)(*parts)

    outer = zh == zl
    pair = jnp.concatenate([out_first, out_second], axis=1).reshape(2, 4, own_rows, 2 * LANES)
    tokens_here = jnp.where(core == 0, pair[0], pair[1])
    tokens_there = jnp.where(core == 0, pair[1], pair[0])
    out_shared = out_shared.reshape(4, own_rows, LANES)

    def pick(x, ends):
        a, b = jnp.where(ends, x[0], x[1]), jnp.where(ends, x[3], x[2])
        return jnp.concatenate([a, b], axis=0)

    tokens_here = jnp.concatenate([tokens_here, out_shared], axis=2)
    kept = pick(tokens_here, outer)
    from_z = flip(pick(tokens_here, ~outer), "zl")
    from_c = flip(pick(tokens_there, outer), "c")
    from_zc = flip(pick(tokens_there, ~outer), "zl", "c")

    def features(own, other):
        w = 2 * LANES
        lo = jnp.where(core == 0, own[:, :w], other)
        hi = jnp.where(core == 0, other, own[:, :w])
        return jnp.concatenate([lo, hi, own[:, w:]], axis=1)

    my_group, next_group = features(kept, from_c), features(from_z, from_zc)
    same = zl == core
    for_own = jnp.where(same, my_group, next_group)
    for_other = jnp.where(same, next_group, my_group)
    partial = jnp.dot(for_own, out_weight, preferred_element_type=F32) + jnp.dot(
        for_other, other_weight, preferred_element_type=F32
    )
    low, high = partial[:own_rows], partial[own_rows:]
    theirs = jnp.where(zh == 0, high, low).astype(BF16)
    ours = jnp.where(zh == 0, low, high)
    projected = ours + flip(theirs, "zh", "zl").astype(F32)
    return (residual.astype(F32) + gate_scale * projected).astype(BF16)


def solution(mesh):
    fine = Mesh(mesh.devices.reshape(tuple(SIZES.values())), ALL)
    tokens = P(ALL, None)
    return jax.shard_map(
        on_device,
        mesh=fine,
        in_specs=(tokens, tokens, tokens, tokens, P(("zh", "c"), None), P()),
        out_specs=tokens,
        check_vma=False,
    )
```

time: 958 us -> 196 us (0.20)
  waiting for transfers between devices: 679 us -> 37.3 us
  matrix products: 122 us -> 6.69 us
  local copies, waits for them, and re-layouts: 90.2 us -> 3.22 us
  starting transfers between devices: 19.2 us -> 78.5 us
  Pallas kernels: 0 us -> 53.8 us
  other arithmetic: 27 us -> 3 us
  between operations: 13.5 us -> 0.39 us
  blocking collectives: 0 us -> 11.9 us
    ppermute x62 -> x34, waiting for transfers between devices: 573 us -> 37.3 us  [move(): return lax.ppermute(x, ALL, pairs)]
    dot_general x65 -> x2, matrix products: 122 us -> 6.69 us  [the longest x1 4.85 us: on_device(): jnp.dot(for_other, other_weight, preferred_element_type=F32)]
    while x157 -> x0, local copies, waits for them, and re-layouts: 83 us -> none
    reduce_scatter x1 -> x0, waiting for transfers between devices: 82.3 us -> none  [on_device(): lax.psum_scatter(jnp.dot(attended, out_weight, preferred_element_type=jnp...]
    ppermute x62 -> x34, starting transfers between devices: 2.58 us -> 62.4 us  [move(): return lax.ppermute(x, ALL, pairs)]
    pallas_call x0 -> x8, Pallas kernels: none -> 53.8 us  [the longest x4 41.6 us: flash(): pl.pallas_call(functools.partial(flash_body, n, rows, key_rows), out_shap...]
    all_to_all x3 -> x2, waiting for transfers between devices: 23.9 us -> 0.01 us  [spread(): got = lax.all_to_all(x, axes, split_axis=0, concat_axis=0, tiled=True)]
    reduce_sum x32 -> x0, other arithmetic: 23.8 us -> none  [absorb(): totals = totals * correction + jnp.sum(weights, axis=-1)]
  transfers between devices with their start and end apart: 66 -> 36, of which waited for: 66 -> 9; matrix products, arithmetic and copies ran while one was open for 20% -> 2% of each run, Pallas kernels for 0% -> 26%
where the time goes in v1:
time: 196 us; the launch traced here: 195 us
  starting transfers between devices  78.5 us (40%)
  Pallas kernels  53.8 us (27%)
  waiting for transfers between devices  37.3 us (19%)
  blocking collectives  11.9 us (6%)
  matrix products  6.69 us (3%)
  local copies, waits for them, and re-layouts  3.22 us (2%)
  other arithmetic  3 us (2%)
    ppermute x34, starting transfers between devices, move(): return lax.ppermute(x, ALL, pairs)  62.4 us
    pallas_call x4, Pallas kernels, flash(): pl.pallas_call(functools.partial(flash_body, n, rows, key_rows), out_shap...  41.6 us
    ppermute x34, waiting for transfers between devices, move(): return lax.ppermute(x, ALL, pairs)  37.3 us
    all_to_all x2, starting transfers between devices, spread(): got = lax.all_to_all(x, axes, split_axis=0, concat_axis=0, tiled=True)  16 us
    all_to_all x1, blocking collectives, spread(): got = lax.all_to_all(x, axes, split_axis=0, concat_axis=0, tiled=True)  11.9 us
    dot_general x1, matrix products, on_device(): jnp.dot(for_other, other_weight, preferred_element_type=F32)  4.85 us
  transfers between devices with their start and end apart: 36, of which 9 were waited for; matrix products, arithmetic and copies ran while one was open for 2% of the time, Pallas kernels for 26%

profile of v1, /device:TPU:1, one launch (start us, length us, event | category | flops | bytes accessed | tf_op | source)
XLA Modules:
  0.0 194.8 jit_solution(14955999182106510723)
XLA Ops:
  0.0 2.8 %shard_map.64 = (bf16[4,3,104,128]{3,2,1,0:T(8,128)(2,1)}, bf16[8,3,104,128]{3,2,1,0:T(8,128)(2,1)}, bf16[8,3,104,128]{3,2,1,0:T(8,128)(2,1)}) custom-call(bf16[104,2560]{1,0:T(8,128)(2,1)} %q.1, bf16[104,2560]{1,0:T(8,128)(2,1)} %k.1, bf16[104,2560]{1,0:T(8,128)(2,1)} %v.1), custom_call_target="tpu_custom_call" | custom-call | tf_op jit(solution)/shard_map/pallas_call | solution.py:62
  2.8 11.9 %all_to_all.15 = bf16[4,3,104,128]{3,2,1,0:T(8,128)(2,1)S(1)} all-to-all(bf16[4,3,104,128]{3,2,1,0:T(8,128)(2,1)} %get-tuple-element.18), channel_id=1, replica_groups=mesh['zh'=2,'c'=2,'y'=4,'zl'=2,'x'=4] {'zh','zl'}, dimensions={0} | all-to-all | bytes 638976 | tf_op jit(solution)/shard_map/all_to_all | solution.py:192
  14.8 2.2 %collective-permute-start.9 = (bf16[416,128]{1,0:T(8,128)(2,1)S(1)}, bf16[416,128]{1,0:T(8,128)(2,1)S(1)}, u32[]{:S(2)}, u32[]{:S(2)}) collective-permute-start(bf16[416,128]{1,0:T(8,128)(2,1)S(1)} %slice_bitcast_fusion.1), channel_id=1, source_target_pairs={{0,32},{1,33},{2,34},{3,35},{4,36},{5,37},{6,38},{7,39},{8,40},{9,... | collective-permute-start | bytes 319496 | tf_op jit(solution)/shard_map/ppermute | solution.py:36
  17.0 2.8 %collective-permute-start.15 = (bf16[2,416,128]{2,1,0:T(8,128)(2,1)S(1)}, bf16[2,416,128]{2,1,0:T(8,128)(2,1)S(1)}, u32[]{:S(2)}, u32[]{:S(2)}) collective-permute-start(bf16[2,416,128]{2,1,0:T(8,128)(2,1)S(1)} %slice.129.refs_4_), channel_id=1, source_target_pairs={{0,16},{1,17},{2,18},{3,19},{4,20},{5,21},{6,22},{7,23},{8,24},{9,... | collective-permute-start | bytes 638984 | tf_op jit(solution)/shard_map/ppermute | solution.py:36
  21.3 3.0 %collective-permute-start.12 = (bf16[832,128]{1,0:T(8,128)(2,1)S(1)}, bf16[832,128]{1,0:T(8,128)(2,1)S(1)}, u32[]{:S(2)}, u32[]{:S(2)}) collective-permute-start(bf16[832,128]{1,0:T(8,128)(2,1)S(1)} %pad_maximum_fusion.2.refs_0_), channel_id=1, source_target_pairs={{0,2},{1,3},{2,0},{3,1},{4,6},{5,7},{6,4},{7,5},{8,10},{9,11},{10,... | collective-permute-start | bytes 638984 | tf_op jit(solution)/shard_map/ppermute | solution.py:36
  26.0 1.8 collective-permute-start.32
  27.8 3.5 %all-to-all-start.1 = ((bf16[8,3,104,128]{3,2,1,0:T(8,128)(2,1)}), bf16[8,3,104,128]{3,2,1,0:T(8,128)(2,1)S(1)}, u32[]{:S(2)}, u32[]{:S(2)}) async-start(bf16[8,3,104,128]{3,2,1,0:T(8,128)(2,1)} %get-tuple-element.19), calls=%async_computation.1 | async-start | bytes 1277952 | tf_op jit(solution)/shard_map/all_to_all | solution.py:192
  32.6 9.6 %shard_map.66 = bf16[8,432,128]{2,1,0:T(8,128)(2,1)S(1)} custom-call(bf16[832,128]{1,0:T(8,128)(2,1)S(1)} %pad_maximum_fusion.2.refs_0_, bf16[832,128]{1,0:T(8,128)(2,1)S(1)} %collective-permute-done.10.refs_1_, bf16[832,128]{1,0:T(8,128)(2,1)S(1)} %collective-permute-done.11.refs_2_, bf16[832,128]{1,0:T(8,128)(2,1)S(1)} %collective-permute-done.12.refs_3_, ...), custom_call_target="tpu_custom_call" | custom-call | flops 5670699008 | bytes 3407872 | tf_op jit(solution)/shard_map/pallas_call | solution.py:141
  42.9 2.0 %collective-permute-start.18 = (bf16[2,432,128]{2,1,0:T(8,128)(2,1)S(1)}, bf16[2,432,128]{2,1,0:T(8,128)(2,1)S(1)}, u32[]{:S(2)}, u32[]{:S(2)}) collective-permute-start(bf16[2,432,128]{2,1,0:T(8,128)(2,1)S(1)} %get-tuple-element.29), channel_id=1, source_target_pairs={{0,2},{1,3},{2,0},{3,1},{4,6},{5,7},{6,4},{7,5},{8,10},{9,11},{10,... | collective-permute-start | bytes 663560 | tf_op jit(solution)/shard_map/ppermute | solution.py:36
  45.0 1.6 collective-permute-start.17
  49.5 3.1 %collective-permute-start.1 = (bf16[832,128]{1,0:T(8,128)(2,1)S(1)}, bf16[832,128]{1,0:T(8,128)(2,1)S(1)}, u32[]{:S(2)}, u32[]{:S(2)}) collective-permute-start(bf16[832,128]{1,0:T(8,128)(2,1)S(1)} %slice_bitcast_fusion.refs_0_), channel_id=1, source_target_pairs={{0,3},{1,0},{2,1},{3,2},{4,7},{5,4},{6,5},{7,6},{8,11},{9,8},{10,9... | collective-permute-start | bytes 638984 | tf_op jit(solution)/shard_map/ppermute | solution.py:36
  52.6 4.4 %collective-permute-start.5 = (bf16[2,832,128]{2,1,0:T(8,128)(2,1)S(1)}, bf16[2,832,128]{2,1,0:T(8,128)(2,1)S(1)}, u32[]{:S(2)}, u32[]{:S(2)}) collective-permute-start(bf16[2,832,128]{2,1,0:T(8,128)(2,1)S(1)} %slice.123.refs_4_), channel_id=1, source_target_pairs={{0,16},{1,17},{2,18},{3,19},{4,20},{5,21},{6,22},{7,23},{8,24},{9,... | collective-permute-start | bytes 1277960 | tf_op jit(solution)/shard_map/ppermute | solution.py:36
  58.5 3.2 %shard_map.67 = (bf16[1,432,128]{2,1,0:T(8,128)(2,1)}, bf16[1,432,128]{2,1,0:T(8,128)(2,1)}) custom-call(bf16[2,432,128]{2,1,0:T(8,128)(2,1)} %get-tuple-element.32.a, bf16[2,432,128]{2,1,0:T(8,128)(2,1)} %collective-permute-done.16.b, bf16[2,432,128]{2,1,0:T(8,128)(2,1)} %copy-done.4, bf16[2,432,128]{2,1,0:T(8,128)(2,1)} %copy-done.3), custom_call_target="tpu_custom_call" | custom-call | tf_op jit(solution)/shard_map/pallas_call | solution.py:214
  61.7 12.5 %all-to-all-start.2 = ((bf16[8,3,104,128]{3,2,1,0:T(8,128)(2,1)}), bf16[8,3,104,128]{3,2,1,0:T(8,128)(2,1)S(1)}, u32[]{:S(2)}, u32[]{:S(2)}) async-start(bf16[8,3,104,128]{3,2,1,0:T(8,128)(2,1)} %get-tuple-element.25), calls=%async_computation.2 | async-start | bytes 1277952 | tf_op jit(solution)/shard_map/all_to_all | solution.py:192
  74.3 15.8 %shard_map.65 = bf16[8,432,128]{2,1,0:T(8,128)(2,1)S(1)} custom-call(bf16[832,128]{1,0:T(8,128)(2,1)S(1)} %slice_bitcast_fusion.refs_0_, bf16[832,128]{1,0:T(8,128)(2,1)S(1)} %collective-permute-done.refs_1_, bf16[832,128]{1,0:T(8,128)(2,1)S(1)} %collective-permute-done.1.refs_2_, bf16[832,128]{1,0:T(8,128)(2,1)S(1)} %collective-permute-done.2.refs_3_, ...), custom_call_target="tpu_custom_call" | custom-call | flops 11341398016 | bytes 3407872 | tf_op jit(solution)/shard_map/pallas_call | solution.py:141
  90.9 1.7 collective-permute-start.8
  92.6 3.2 %collective-permute-start.7 = (bf16[2,432,128]{2,1,0:T(8,128)(2,1)S(1)}, bf16[2,432,128]{2,1,0:T(8,128)(2,1)S(1)}, u32[]{:S(2)}, u32[]{:S(2)}) collective-permute-start(bf16[2,432,128]{2,1,0:T(8,128)(2,1)S(1)} %get-tuple-element.34), channel_id=1, source_target_pairs={{0,1},{1,2},{2,3},{3,0},{4,5},{5,6},{6,7},{7,4},{8,9},{9,10},{10,1... | collective-permute-start | bytes 663560 | tf_op jit(solution)/shard_map/ppermute | solution.py:36
  95.9 1.9 collective-permute-start.25
  97.8 3.8 %collective-permute-start.24 = (bf16[832,128]{1,0:T(8,128)(2,1)S(1)}, bf16[832,128]{1,0:T(8,128)(2,1)S(1)}, u32[]{:S(2)}, u32[]{:S(2)}) collective-permute-start(bf16[832,128]{1,0:T(8,128)(2,1)S(1)} %bitcast.29), channel_id=1, source_target_pairs={{0,3},{1,0},{2,1},{3,2},{4,7},{5,4},{6,5},{7,6},{8,11},{9,8},{10,9... | collective-permute-start | bytes 638984 | tf_op jit(solution)/shard_map/ppermute | solution.py:36
  101.6 4.9 %collective-permute-start.22 = (bf16[2,832,128]{2,1,0:T(8,128)(2,1)S(1)}, bf16[2,832,128]{2,1,0:T(8,128)(2,1)S(1)}, u32[]{:S(2)}, u32[]{:S(2)}) collective-permute-start(bf16[2,832,128]{2,1,0:T(8,128)(2,1)S(1)} %bitcast.23), channel_id=1, source_target_pairs={{0,16},{1,17},{2,18},{3,19},{4,20},{5,21},{6,22},{7,23},{8,24},{9,... | collective-permute-start | bytes 1277960 | tf_op jit(solution)/shard_map/ppermute | solution.py:36
  108.0 3.3 %shard_map.68 = (bf16[832,128]{1,0:T(8,128)(2,1)}, bf16[416,128]{1,0:T(8,128)(2,1)}) custom-call(bf16[2,432,128]{2,1,0:T(8,128)(2,1)} %get-tuple-element.36.a, bf16[2,432,128]{2,1,0:T(8,128)(2,1)} %copy-done.10, bf16[2,432,128]{2,1,0:T(8,128)(2,1)} %copy-done.9, bf16[2,432,128]{2,1,0:T(8,128)(2,1)} %copy-done.8, ...), custom_call_target="tpu_custom_call" | custom-call | tf_op jit(solution)/shard_map/pallas_call | solution.py:224
  111.3 4.3 %collective-permute-done.23.refs_0_ = bf16[832,128]{1,0:T(8,128)(2,1)S(1)} collective-permute-done((bf16[832,128]{1,0:T(8,128)(2,1)S(1)}, bf16[832,128]{1,0:T(8,128)(2,1)S(1)}, u32[]{:S(2)}, u32[]{:S(2)}) %collective-permute-start.23) | collective-permute-done | bytes 213024 | tf_op jit(solution)/shard_map/ppermute | solution.py:36
  116.7 12.0 %shard_map.70 = bf16[6,432,128]{2,1,0:T(8,128)(2,1)S(1)} custom-call(bf16[832,128]{1,0:T(8,128)(2,1)S(1)} %collective-permute-done.23.refs_0_, bf16[832,128]{1,0:T(8,128)(2,1)S(1)} %collective-permute-done.24.refs_1_, bf16[832,128]{1,0:T(8,128)(2,1)S(1)} %collective-permute-done.25.refs_2_, bf16[2,832,128]{2,1,0:T(8,128)(2,1)S(1)} %bitcast.26, ...), custom_call_target="tpu_custom_call" | custom-call | flops 8506048512 | bytes 2555904 | tf_op jit(solution)/shard_map/pallas_call | solution.py:141
  129.9 3.6 %collective-permute-start.27 = (bf16[2,432,128]{2,1,0:T(8,128)(2,1)S(1)}, bf16[2,432,128]{2,1,0:T(8,128)(2,1)S(1)}, u32[]{:S(2)}, u32[]{:S(2)}) collective-permute-start(bf16[2,432,128]{2,1,0:T(8,128)(2,1)S(1)} %get-tuple-element.38), channel_id=1, source_target_pairs={{0,1},{1,2},{2,3},{3,0},{4,5},{5,6},{6,7},{7,4},{8,9},{9,10},{10,1... | collective-permute-start | bytes 663560 | tf_op jit(solution)/shard_map/ppermute | solution.py:36
  133.5 4.2 %shard_map.69.a = bf16[2,432,128]{2,1,0:T(8,128)(2,1)S(1)} custom-call(bf16[832,128]{1,0:T(8,128)(2,1)S(1)} %bitcast.31, bf16[2,832,128]{2,1,0:T(8,128)(2,1)S(1)} %bitcast.27, bf16[2,832,128]{2,1,0:T(8,128)(2,1)S(1)} %collective-permute-done.20.refs_2_.refs_4_, bf16[2,832,128]{2,1,0:T(8,128)(2,1)S(1)} %collective-permute-done.21.refs_3_.refs_5_, ...), custom_call_target="tpu_custom_call" | custom-call | flops 2835349504 | bytes 851968 | tf_op jit(solution)/shard_map/pallas_call | solution.py:141
  139.9 3.0 %shard_map.71 = bf16[832,128]{1,0:T(8,128)(2,1)} custom-call(bf16[2,432,128]{2,1,0:T(8,128)(2,1)} %copy-done, bf16[2,432,128]{2,1,0:T(8,128)(2,1)} %copy-done.7, bf16[2,432,128]{2,1,0:T(8,128)(2,1)} %copy-done.6, bf16[2,432,128]{2,1,0:T(8,128)(2,1)} %copy-done.5), custom_call_target="tpu_custom_call" | custom-call | tf_op jit(solution)/shard_map/pallas_call | solution.py:233
  144.1 10.7 %collective-permute-start.31 = (bf16[208,256]{1,0:T(8,128)(2,1)S(1)}, bf16[208,256]{1,0:T(8,128)(2,1)S(1)}, u32[]{:S(2)}, u32[]{:S(2)}) collective-permute-start(bf16[208,256]{1,0:T(8,128)(2,1)S(1)} %pad_maximum_fusion.7), channel_id=1, source_target_pairs={{0,36},{1,37},{2,38},{3,39},{4,32},{5,33},{6,34},{7,35},{8,44},{9,... | collective-permute-start | bytes 319496 | tf_op jit(solution)/shard_map/ppermute | solution.py:36
  156.2 4.9 %collective-permute-done.30 = bf16[208,384]{1,0:T(8,128)(2,1)S(1)} collective-permute-done((bf16[208,384]{1,0:T(8,128)(2,1)S(1)}, bf16[208,384]{1,0:T(8,128)(2,1)S(1)}, u32[]{:S(2)}, u32[]{:S(2)}) %collective-permute-start.30) | collective-permute-done | bytes 159776 | tf_op jit(solution)/shard_map/ppermute | solution.py:36
  161.2 4.9 %fusion.4 = f32[208,5120]{1,0:T(8,128)S(1)} fusion(bf16[640,5120]{1,0:T(8,128)(2,1)} %collective-permute-done.32, pred[]{:T(512)S(6)} %eq.9, bf16[208,128]{1,0:T(8,128)(2,1)S(1)} %slice.184, bf16[208,256]{1,0:T(8,128)(2,1)S(1)} %get-tuple-element.48, bf16[208,256]{1,0:T(8,128)(2,1)S(1)} %get-tuple-element.47, bf16[104,384]{1,0:T(8,128)(2,1)S(1)} %get-tuple-element.27, ...), kind=kOutput, calls=%fused_computation.17 | convolution fusion | flops 1365544960 | bytes 11452417 | tf_op jit(solution)/shard_map/dot_general | solution.py:261
  166.0 1.8 convolution_add_fusion
  168.1 2.3 %collective-permute-start.33 = (bf16[104,5120]{1,0:T(8,128)(2,1)S(1)}, bf16[104,5120]{1,0:T(8,128)(2,1)S(1)}, u32[]{:S(2)}, u32[]{:S(2)}) collective-permute-start(bf16[104,5120]{1,0:T(8,128)(2,1)S(1)} %select_convert_fusion), channel_id=1, source_target_pairs={{0,68},{1,69},{2,70},{3,71},{4,64},{5,65},{6,66},{7,67},{8,76},{9,... | collective-permute-start | bytes 3194888 | tf_op jit(solution)/shard_map/ppermute | solution.py:36
  170.4 22.9 %collective-permute-done.33 = bf16[104,5120]{1,0:T(8,128)(2,1)S(1)} collective-permute-done((bf16[104,5120]{1,0:T(8,128)(2,1)S(1)}, bf16[104,5120]{1,0:T(8,128)(2,1)S(1)}, u32[]{:S(2)}, u32[]{:S(2)}) %collective-permute-start.33) | collective-permute-done | bytes 1064992 | tf_op jit(solution)/shard_map/ppermute | solution.py:36
  (107 shorter events, 20.9 us)
Async XLA Ops:
  14.8 6.6 %collective-permute-start.9 = (bf16[416,128]{1,0:T(8,128)(2,1)S(1)}, bf16[416,128]{1,0:T(8,128)(2,1)S(1)}, u32[]{:S(2)}, u32[]{:S(2)}) collective-permute-start(bf16[416,128]{1,0:T(8,128)(2,1)S(1)} %slice_bitcast_fusion.1), channel_id=1, source_target_pairs={{0,32},{1,33},{2,34},{3,35},{4,36},{5,37},{6,38},{7,39},{8,40},{9,... | collective-permute-start | bytes 319496 | tf_op jit(solution)/shard_map/ppermute | solution.py:36
  17.0 8.1 %collective-permute-start.15 = (bf16[2,416,128]{2,1,0:T(8,128)(2,1)S(1)}, bf16[2,416,128]{2,1,0:T(8,128)(2,1)S(1)}, u32[]{:S(2)}, u32[]{:S(2)}) collective-permute-start(bf16[2,416,128]{2,1,0:T(8,128)(2,1)S(1)} %slice.129.refs_4_), channel_id=1, source_target_pairs={{0,16},{1,17},{2,18},{3,19},{4,20},{5,21},{6,22},{7,23},{8,24},{9,... | collective-permute-start | bytes 638984 | tf_op jit(solution)/shard_map/ppermute | solution.py:36
  20.7 10.6 %collective-permute-start.13 = (bf16[2,416,128]{2,1,0:T(8,128)(2,1)S(1)}, bf16[2,416,128]{2,1,0:T(8,128)(2,1)S(1)}, u32[]{:S(2)}, u32[]{:S(2)}) collective-permute-start(bf16[2,416,128]{2,1,0:T(8,128)(2,1)S(1)} %slice.129.refs_4_), channel_id=1, source_target_pairs={{0,8},{1,9},{2,10},{3,11},{4,12},{5,13},{6,14},{7,15},{8,16},{9,17... | collective-permute-start | bytes 638984 | tf_op jit(solution)/shard_map/ppermute | solution.py:36
  21.3 9.9 %collective-permute-start.12 = (bf16[832,128]{1,0:T(8,128)(2,1)S(1)}, bf16[832,128]{1,0:T(8,128)(2,1)S(1)}, u32[]{:S(2)}, u32[]{:S(2)}) collective-permute-start(bf16[832,128]{1,0:T(8,128)(2,1)S(1)} %pad_maximum_fusion.2.refs_0_), channel_id=1, source_target_pairs={{0,2},{1,3},{2,0},{3,1},{4,6},{5,7},{6,4},{7,5},{8,10},{9,11},{10,... | collective-permute-start | bytes 638984 | tf_op jit(solution)/shard_map/ppermute | solution.py:36
  24.3 7.0 %collective-permute-start.11 = (bf16[832,128]{1,0:T(8,128)(2,1)S(1)}, bf16[832,128]{1,0:T(8,128)(2,1)S(1)}, u32[]{:S(2)}, u32[]{:S(2)}) collective-permute-start(bf16[832,128]{1,0:T(8,128)(2,1)S(1)} %pad_maximum_fusion.2.refs_0_), channel_id=1, source_target_pairs={{0,3},{1,0},{2,1},{3,2},{4,7},{5,4},{6,5},{7,6},{8,11},{9,8},{10,9... | collective-permute-start | bytes 638984 | tf_op jit(solution)/shard_map/ppermute | solution.py:36
  25.1 7.5 %collective-permute-start.10 = (bf16[832,128]{1,0:T(8,128)(2,1)S(1)}, bf16[832,128]{1,0:T(8,128)(2,1)S(1)}, u32[]{:S(2)}, u32[]{:S(2)}) collective-permute-start(bf16[832,128]{1,0:T(8,128)(2,1)S(1)} %pad_maximum_fusion.2.refs_0_), channel_id=1, source_target_pairs={{0,1},{1,2},{2,3},{3,0},{4,5},{5,6},{6,7},{7,4},{8,9},{9,10},{10,1... | collective-permute-start | bytes 638984 | tf_op jit(solution)/shard_map/ppermute | solution.py:36
  26.0 135.2 %collective-permute-start.32 = (bf16[640,5120]{1,0:T(8,128)(2,1)}, bf16[640,5120]{1,0:T(8,128)(2,1)}, u32[]{:S(2)}, u32[]{:S(2)}) collective-permute-start(bf16[640,5120]{1,0:T(8,128)(2,1)} %param.10), channel_id=1, source_target_pairs={{0,32},{1,33},{2,34},{3,35},{4,36},{5,37},{6,38},{7,39},{8,40},{9,... | collective-permute-start | bytes 19660808 | tf_op jit(solution)/shard_map/ppermute | solution.py:36
  27.8 19.9 %all-to-all-start.1 = ((bf16[8,3,104,128]{3,2,1,0:T(8,128)(2,1)}), bf16[8,3,104,128]{3,2,1,0:T(8,128)(2,1)S(1)}, u32[]{:S(2)}, u32[]{:S(2)}) async-start(bf16[8,3,104,128]{3,2,1,0:T(8,128)(2,1)} %get-tuple-element.19), calls=%async_computation.1 | async-start | bytes 1277952 | tf_op jit(solution)/shard_map/all_to_all | solution.py:192
  42.9 6.6 %collective-permute-start.18 = (bf16[2,432,128]{2,1,0:T(8,128)(2,1)S(1)}, bf16[2,432,128]{2,1,0:T(8,128)(2,1)S(1)}, u32[]{:S(2)}, u32[]{:S(2)}) collective-permute-start(bf16[2,432,128]{2,1,0:T(8,128)(2,1)S(1)} %get-tuple-element.29), channel_id=1, source_target_pairs={{0,2},{1,3},{2,0},{3,1},{4,6},{5,7},{6,4},{7,5},{8,10},{9,11},{10,... | collective-permute-start | bytes 663560 | tf_op jit(solution)/shard_map/ppermute | solution.py:36
  45.0 7.6 %collective-permute-start.17 = (bf16[2,432,128]{2,1,0:T(8,128)(2,1)S(1)}, bf16[2,432,128]{2,1,0:T(8,128)(2,1)S(1)}, u32[]{:S(2)}, u32[]{:S(2)}) collective-permute-start(bf16[2,432,128]{2,1,0:T(8,128)(2,1)S(1)} %get-tuple-element.30), channel_id=1, source_target_pairs={{0,1},{1,2},{2,3},{3,0},{4,5},{5,6},{6,7},{7,4},{8,9},{9,10},{10,1... | collective-permute-start | bytes 663560 | tf_op jit(solution)/shard_map/ppermute | solution.py:36
  46.6 10.5 %collective-permute-start.16 = (bf16[2,432,128]{2,1,0:T(8,128)(2,1)S(1)}, bf16[2,432,128]{2,1,0:T(8,128)(2,1)}, u32[]{:S(2)}, u32[]{:S(2)}) collective-permute-start(bf16[2,432,128]{2,1,0:T(8,128)(2,1)S(1)} %get-tuple-element.31), channel_id=1, source_target_pairs={{0,3},{1,0},{2,1},{3,2},{4,7},{5,4},{6,5},{7,6},{8,11},{9,8},{10,9... | collective-permute-start | bytes 663560 | tf_op jit(solution)/shard_map/ppermute | solution.py:36
  47.7 9.3 %collective-permute-start.2 = (bf16[832,128]{1,0:T(8,128)(2,1)S(1)}, bf16[832,128]{1,0:T(8,128)(2,1)S(1)}, u32[]{:S(2)}, u32[]{:S(2)}) collective-permute-start(bf16[832,128]{1,0:T(8,128)(2,1)S(1)} %slice_bitcast_fusion.refs_0_), channel_id=1, source_target_pairs={{0,2},{1,3},{2,0},{3,1},{4,6},{5,7},{6,4},{7,5},{8,10},{9,11},{10,... | collective-permute-start | bytes 638984 | tf_op jit(solution)/shard_map/ppermute | solution.py:36
  49.5 9.0 %collective-permute-start.1 = (bf16[832,128]{1,0:T(8,128)(2,1)S(1)}, bf16[832,128]{1,0:T(8,128)(2,1)S(1)}, u32[]{:S(2)}, u32[]{:S(2)}) collective-permute-start(bf16[832,128]{1,0:T(8,128)(2,1)S(1)} %slice_bitcast_fusion.refs_0_), channel_id=1, source_target_pairs={{0,3},{1,0},{2,1},{3,2},{4,7},{5,4},{6,5},{7,6},{8,11},{9,8},{10,9... | collective-permute-start | bytes 638984 | tf_op jit(solution)/shard_map/ppermute | solution.py:36
  52.6 21.7 %collective-permute-start.5 = (bf16[2,832,128]{2,1,0:T(8,128)(2,1)S(1)}, bf16[2,832,128]{2,1,0:T(8,128)(2,1)S(1)}, u32[]{:S(2)}, u32[]{:S(2)}) collective-permute-start(bf16[2,832,128]{2,1,0:T(8,128)(2,1)S(1)} %slice.123.refs_4_), channel_id=1, source_target_pairs={{0,16},{1,17},{2,18},{3,19},{4,20},{5,21},{6,22},{7,23},{8,24},{9,... | collective-permute-start | bytes 1277960 | tf_op jit(solution)/shard_map/ppermute | solution.py:36
  57.0 17.3 %collective-permute-start.4 = (bf16[2,832,128]{2,1,0:T(8,128)(2,1)S(1)}, bf16[2,832,128]{2,1,0:T(8,128)(2,1)S(1)}, u32[]{:S(2)}, u32[]{:S(2)}) collective-permute-start(bf16[2,832,128]{2,1,0:T(8,128)(2,1)S(1)} %slice.123.refs_4_), channel_id=1, source_target_pairs={{0,24},{1,25},{2,26},{3,27},{4,28},{5,29},{6,30},{7,31},{8,0},{9,1... | collective-permute-start | bytes 1277960 | tf_op jit(solution)/shard_map/ppermute | solution.py:36
  57.0 17.3 %collective-permute-start.3 = (bf16[2,832,128]{2,1,0:T(8,128)(2,1)S(1)}, bf16[2,832,128]{2,1,0:T(8,128)(2,1)S(1)}, u32[]{:S(2)}, u32[]{:S(2)}) collective-permute-start(bf16[2,832,128]{2,1,0:T(8,128)(2,1)S(1)} %slice.123.refs_4_), channel_id=1, source_target_pairs={{0,8},{1,9},{2,10},{3,11},{4,12},{5,13},{6,14},{7,15},{8,16},{9,17... | collective-permute-start | bytes 1277960 | tf_op jit(solution)/shard_map/ppermute | solution.py:36
  58.5 15.7 %collective-permute-start = (bf16[832,128]{1,0:T(8,128)(2,1)S(1)}, bf16[832,128]{1,0:T(8,128)(2,1)S(1)}, u32[]{:S(2)}, u32[]{:S(2)}) collective-permute-start(bf16[832,128]{1,0:T(8,128)(2,1)S(1)} %slice_bitcast_fusion.refs_0_), channel_id=1, source_target_pairs={{0,1},{1,2},{2,3},{3,0},{4,5},{5,6},{6,7},{7,4},{8,9},{9,10},{10,1... | collective-permute-start | bytes 638984 | tf_op jit(solution)/shard_map/ppermute | solution.py:36
  61.7 34.1 %all-to-all-start.2 = ((bf16[8,3,104,128]{3,2,1,0:T(8,128)(2,1)}), bf16[8,3,104,128]{3,2,1,0:T(8,128)(2,1)S(1)}, u32[]{:S(2)}, u32[]{:S(2)}) async-start(bf16[8,3,104,128]{3,2,1,0:T(8,128)(2,1)} %get-tuple-element.25), calls=%async_computation.2 | async-start | bytes 1277952 | tf_op jit(solution)/shard_map/all_to_all | solution.py:192
  74.2 21.6 %collective-permute-start.19 = (bf16[1,432,128]{2,1,0:T(8,128)(2,1)}, bf16[1,432,128]{2,1,0:T(8,128)(2,1)}, u32[]{:S(2)}, u32[]{:S(2)}) collective-permute-start(bf16[1,432,128]{2,1,0:T(8,128)(2,1)} %get-tuple-element.23), channel_id=1, source_target_pairs={{0,32},{1,33},{2,34},{3,35},{4,36},{5,37},{6,38},{7,39},{8,40},{9,... | collective-permute-start | bytes 331784 | tf_op jit(solution)/shard_map/ppermute | solution.py:36
  90.9 6.9 %collective-permute-start.8 = (bf16[2,432,128]{2,1,0:T(8,128)(2,1)S(1)}, bf16[2,432,128]{2,1,0:T(8,128)(2,1)S(1)}, u32[]{:S(2)}, u32[]{:S(2)}) collective-permute-start(bf16[2,432,128]{2,1,0:T(8,128)(2,1)S(1)} %get-tuple-element.33), channel_id=1, source_target_pairs={{0,2},{1,3},{2,0},{3,1},{4,6},{5,7},{6,4},{7,5},{8,10},{9,11},{10,... | collective-permute-start | bytes 663560 | tf_op jit(solution)/shard_map/ppermute | solution.py:36
  92.6 9.0 %collective-permute-start.7 = (bf16[2,432,128]{2,1,0:T(8,128)(2,1)S(1)}, bf16[2,432,128]{2,1,0:T(8,128)(2,1)S(1)}, u32[]{:S(2)}, u32[]{:S(2)}) collective-permute-start(bf16[2,432,128]{2,1,0:T(8,128)(2,1)S(1)} %get-tuple-element.34), channel_id=1, source_target_pairs={{0,1},{1,2},{2,3},{3,0},{4,5},{5,6},{6,7},{7,4},{8,9},{9,10},{10,1... | collective-permute-start | bytes 663560 | tf_op jit(solution)/shard_map/ppermute | solution.py:36
  95.8 10.7 %collective-permute-start.6 = (bf16[2,432,128]{2,1,0:T(8,128)(2,1)S(1)}, bf16[2,432,128]{2,1,0:T(8,128)(2,1)S(1)}, u32[]{:S(2)}, u32[]{:S(2)}) collective-permute-start(bf16[2,432,128]{2,1,0:T(8,128)(2,1)S(1)} %get-tuple-element.35), channel_id=1, source_target_pairs={{0,3},{1,0},{2,1},{3,2},{4,7},{5,4},{6,5},{7,6},{8,11},{9,8},{10,9... | collective-permute-start | bytes 663560 | tf_op jit(solution)/shard_map/ppermute | solution.py:36
  95.9 10.7 %collective-permute-start.25 = (bf16[832,128]{1,0:T(8,128)(2,1)S(1)}, bf16[832,128]{1,0:T(8,128)(2,1)S(1)}, u32[]{:S(2)}, u32[]{:S(2)}) collective-permute-start(bf16[832,128]{1,0:T(8,128)(2,1)S(1)} %bitcast.28), channel_id=1, source_target_pairs={{0,2},{1,3},{2,0},{3,1},{4,6},{5,7},{6,4},{7,5},{8,10},{9,11},{10,... | collective-permute-start | bytes 638984 | tf_op jit(solution)/shard_map/ppermute | solution.py:36
  97.8 10.2 %collective-permute-start.24 = (bf16[832,128]{1,0:T(8,128)(2,1)S(1)}, bf16[832,128]{1,0:T(8,128)(2,1)S(1)}, u32[]{:S(2)}, u32[]{:S(2)}) collective-permute-start(bf16[832,128]{1,0:T(8,128)(2,1)S(1)} %bitcast.29), channel_id=1, source_target_pairs={{0,3},{1,0},{2,1},{3,2},{4,7},{5,4},{6,5},{7,6},{8,11},{9,8},{10,9... | collective-permute-start | bytes 638984 | tf_op jit(solution)/shard_map/ppermute | solution.py:36
  101.6 13.9 %collective-permute-start.22 = (bf16[2,832,128]{2,1,0:T(8,128)(2,1)S(1)}, bf16[2,832,128]{2,1,0:T(8,128)(2,1)S(1)}, u32[]{:S(2)}, u32[]{:S(2)}) collective-permute-start(bf16[2,832,128]{2,1,0:T(8,128)(2,1)S(1)} %bitcast.23), channel_id=1, source_target_pairs={{0,16},{1,17},{2,18},{3,19},{4,20},{5,21},{6,22},{7,23},{8,24},{9,... | collective-permute-start | bytes 1277960 | tf_op jit(solution)/shard_map/ppermute | solution.py:36
  106.5 10.2 %collective-permute-start.21 = (bf16[2,832,128]{2,1,0:T(8,128)(2,1)S(1)}, bf16[2,832,128]{2,1,0:T(8,128)(2,1)S(1)}, u32[]{:S(2)}, u32[]{:S(2)}) collective-permute-start(bf16[2,832,128]{2,1,0:T(8,128)(2,1)S(1)} %bitcast.24), channel_id=1, source_target_pairs={{0,24},{1,25},{2,26},{3,27},{4,28},{5,29},{6,30},{7,31},{8,0},{9,1... | collective-permute-start | bytes 1277960 | tf_op jit(solution)/shard_map/ppermute | solution.py:36
  106.5 10.2 %collective-permute-start.20 = (bf16[2,832,128]{2,1,0:T(8,128)(2,1)S(1)}, bf16[2,832,128]{2,1,0:T(8,128)(2,1)S(1)}, u32[]{:S(2)}, u32[]{:S(2)}) collective-permute-start(bf16[2,832,128]{2,1,0:T(8,128)(2,1)S(1)} %bitcast.25), channel_id=1, source_target_pairs={{0,8},{1,9},{2,10},{3,11},{4,12},{5,13},{6,14},{7,15},{8,16},{9,17... | collective-permute-start | bytes 1277960 | tf_op jit(solution)/shard_map/ppermute | solution.py:36
  108.0 7.6 %collective-permute-start.23 = (bf16[832,128]{1,0:T(8,128)(2,1)S(1)}, bf16[832,128]{1,0:T(8,128)(2,1)S(1)}, u32[]{:S(2)}, u32[]{:S(2)}) collective-permute-start(bf16[832,128]{1,0:T(8,128)(2,1)S(1)} %bitcast.30), channel_id=1, source_target_pairs={{0,1},{1,2},{2,3},{3,0},{4,5},{5,6},{6,7},{7,4},{8,9},{9,10},{10,1... | collective-permute-start | bytes 638984 | tf_op jit(solution)/shard_map/ppermute | solution.py:36
  128.7 9.6 %collective-permute-start.28 = (bf16[2,432,128]{2,1,0:T(8,128)(2,1)S(1)}, bf16[2,432,128]{2,1,0:T(8,128)(2,1)S(1)}, u32[]{:S(2)}, u32[]{:S(2)}) collective-permute-start(bf16[2,432,128]{2,1,0:T(8,128)(2,1)S(1)} %get-tuple-element.37), channel_id=1, source_target_pairs={{0,2},{1,3},{2,0},{3,1},{4,6},{5,7},{6,4},{7,5},{8,10},{9,11},{10,... | collective-permute-start | bytes 663560 | tf_op jit(solution)/shard_map/ppermute | solution.py:36
  129.9 8.5 %collective-permute-start.27 = (bf16[2,432,128]{2,1,0:T(8,128)(2,1)S(1)}, bf16[2,432,128]{2,1,0:T(8,128)(2,1)S(1)}, u32[]{:S(2)}, u32[]{:S(2)}) collective-permute-start(bf16[2,432,128]{2,1,0:T(8,128)(2,1)S(1)} %get-tuple-element.38), channel_id=1, source_target_pairs={{0,1},{1,2},{2,3},{3,0},{4,5},{5,6},{6,7},{7,4},{8,9},{9,10},{10,1... | collective-permute-start | bytes 663560 | tf_op jit(solution)/shard_map/ppermute | solution.py:36
  144.1 17.0 %collective-permute-start.31 = (bf16[208,256]{1,0:T(8,128)(2,1)S(1)}, bf16[208,256]{1,0:T(8,128)(2,1)S(1)}, u32[]{:S(2)}, u32[]{:S(2)}) collective-permute-start(bf16[208,256]{1,0:T(8,128)(2,1)S(1)} %pad_maximum_fusion.7), channel_id=1, source_target_pairs={{0,36},{1,37},{2,38},{3,39},{4,32},{5,33},{6,34},{7,35},{8,44},{9,... | collective-permute-start | bytes 319496 | tf_op jit(solution)/shard_map/ppermute | solution.py:36
  168.1 25.2 %collective-permute-start.33 = (bf16[104,5120]{1,0:T(8,128)(2,1)S(1)}, bf16[104,5120]{1,0:T(8,128)(2,1)S(1)}, u32[]{:S(2)}, u32[]{:S(2)}) collective-permute-start(bf16[104,5120]{1,0:T(8,128)(2,1)S(1)} %select_convert_fusion), channel_id=1, source_target_pairs={{0,68},{1,69},{2,70},{3,71},{4,64},{5,65},{6,66},{7,67},{8,76},{9,... | collective-permute-start | bytes 3194888 | tf_op jit(solution)/shard_map/ppermute | solution.py:36
  (19 other events, 148.2 us)

commit v2 on v1

v2 whole, which is shorter than its diff:
```python
import functools

import jax
import jax.numpy as jnp
from jax import lax
from jax.experimental import pallas as pl
from jax.experimental.pallas import tpu as pltpu
from jax.sharding import Mesh
from jax.sharding import PartitionSpec as P

HEAD_DIM = 128
LANES = 128
SCALE = HEAD_DIM**-0.5 * 1.4426950408889634
ALL = ("zh", "c", "y", "zl", "x")
SIZES = {"zh": 2, "c": 2, "y": 4, "zl": 2, "x": 4}
Z = ("zh", "zl")
CZ = ("c", "zh", "zl")
KEY_TILE = 256
LEVEL_ROWS = 16
F32 = jnp.float32
BF16 = jnp.bfloat16
NT = (((1,), (1,)), ((), ()))


def flip(x, *names):
    total = 2 ** len(names)
    return lax.ppermute(x, names, [(i, total - 1 - i) for i in range(total)])


def exchange(x, axes):
    return lax.all_to_all(x, axes, split_axis=0, concat_axis=0, tiled=True)


def gather(x, axis):
    return exchange(jnp.broadcast_to(x[None], (SIZES[axis],) + x.shape), axis)


def cut_body(q, k, v, shared, first, second):
    for i, x in enumerate((q, k, v)):
        for z in range(4):
            for out, heads in ((shared, (4,)), (first, (0, 2)), (second, (1, 3))):
                for c, head in enumerate(heads):
                    lanes = slice((5 * z + head) * LANES, (5 * z + head + 1) * LANES)
                    out[4 * c + z, i] = x[:, lanes]


def cut(q, k, v):
    rows = q.shape[0]
    return pl.pallas_call(
        cut_body,
        out_shape=[jax.ShapeDtypeStruct((n, 3, rows, LANES), BF16) for n in (4, 8, 8)],
    )(q, k, v)


def eye(rows):
    return lax.broadcasted_iota(jnp.int32, (rows, LANES), 0) == lax.broadcasted_iota(
        jnp.int32, (rows, LANES), 1
    )


def write_levels(out, at, level):
    rows = level.shape[0]
    lines = []
    for start in range(0, rows, LANES):
        piece = level[start : start + LANES]
        lines.append(jnp.sum(jnp.where(eye(piece.shape[0]), piece, 0.0), axis=0, keepdims=True))
    line = jnp.concatenate(lines, axis=0)
    high = line.astype(BF16).astype(F32)
    middle = (line - high).astype(BF16).astype(F32)
    low = line - high - middle
    spare = jnp.zeros((LEVEL_ROWS - 3 * len(lines), LANES), F32)
    out[at, rows:, :] = jnp.concatenate([high, middle, low, spare], axis=0).astype(BF16)


def read_levels(block, rows):
    n = -(-rows // LANES)
    parts = block[rows:, :].astype(F32)
    return parts[:n] + parts[n : 2 * n] + parts[2 * n : 3 * n]


def column(line, rows):
    pieces = []
    for i, start in enumerate(range(0, rows, LANES)):
        here = min(LANES, rows - start)
        wide = jnp.broadcast_to(line[i : i + 1], (here, LANES))
        pieces.append(jnp.sum(jnp.where(eye(here), wide, 0.0), axis=1, keepdims=True))
    return jnp.concatenate(pieces, axis=0)


def flash_body(rows, q_ref, kv_ref, out, keys, values):
    key_rows = kv_ref.shape[2]
    values[:, HEAD_DIM:] = jnp.ones((4 * key_rows, LANES), BF16)
    for i in range(4):
        part = pl.ds(i * key_rows, key_rows)
        keys[part, :] = kv_ref[i, 0]
        values[part, :HEAD_DIM] = kv_ref[i, 1]

    def block(i, _):
        q = q_ref[i]
        largest = total = None
        for start in range(0, 4 * key_rows, KEY_TILE):
            part = pl.ds(start, min(KEY_TILE, 4 * key_rows - start))
            scores = lax.dot_general(q, keys[part, :], NT, preferred_element_type=F32)
            new = jnp.max(scores, axis=1, keepdims=True)
            if total is not None:
                new = jnp.maximum(largest, new)
            weights = jnp.exp2((scores - new) * SCALE).astype(BF16)
            update = jnp.dot(weights, values[part, :], preferred_element_type=F32)
            if total is None:
                total = update
            else:
                total = total * jnp.exp2((largest - new) * SCALE) + update
            largest = new
        sums = total[:, HEAD_DIM:]
        result = (total[:, :HEAD_DIM] / sums).astype(BF16)
        level = largest * SCALE + jnp.log2(sums)
        for half in range(2):
            part = slice(half * rows, (half + 1) * rows)
            out[2 * i + half, :rows, :] = result[part]
            write_levels(out, 2 * i + half, level[part])
        return 0

    lax.fori_loop(0, 8, block, 0)


def flash(q, kv):
    rows, key_rows = q.shape[1] // 2, kv.shape[2]
    pairs = 16 * rows * 4 * key_rows
    return pl.pallas_call(
        functools.partial(flash_body, rows),
        out_shape=jax.ShapeDtypeStruct((16, rows + LEVEL_ROWS, LANES), BF16),
        scratch_shapes=[
            pltpu.VMEM((4 * key_rows, HEAD_DIM), BF16),
            pltpu.VMEM((4 * key_rows, 2 * HEAD_DIM), BF16),
        ],
        compiler_params=pltpu.CompilerParams(vmem_limit_bytes=40 << 20),
        cost_estimate=pl.CostEstimate(
            flops=8 * pairs * HEAD_DIM, bytes_accessed=4 << 20, transcendentals=pairs
        ),
    )(q, kv)


def merge_blocks(blocks, rows):
    levels = [read_levels(b, rows) for b in blocks]
    top = functools.reduce(jnp.maximum, levels)
    shares = [jnp.exp2(v - top) for v in levels]
    whole = functools.reduce(jnp.add, shares)
    total = 0.0
    for share, b in zip(shares, blocks):
        total = total + column(share / whole, rows) * b[:rows, :].astype(F32)
    return total.astype(BF16)


def merge_own_body(rows, x, out):
    for z in range(2):
        for c in range(2):
            out[z, c] = merge_blocks([x[4 * i + 2 * c + z] for i in range(4)], rows)


def merge_shared_body(rows, x, out):
    for z in range(2):
        out[z] = merge_blocks([x[4 * i + 2 * c + z] for i in range(4) for c in range(2)], rows)


def merge(body, x, shape):
    return pl.pallas_call(
        functools.partial(body, shape[-2]), out_shape=jax.ShapeDtypeStruct(shape, BF16)
    )(x)


def on_device(query_in, key_in, value_in, residual, out_weight, gate_scale):
    own_rows = query_in.shape[0]
    pair = 2 * own_rows
    other_weight = flip(out_weight, "c")
    zh, core = lax.axis_index("zh"), lax.axis_index("c")

    shared, first, second = cut(query_in, key_in, value_in)

    def spread(x, axes):
        got = exchange(x, axes).transpose(1, 0, 2, 3)
        return got.reshape(3, -1, 4, own_rows, LANES)

    def ordered(q):
        ends_first = jnp.concatenate([q[:, 0:1], q[:, 3:4], q[:, 1:3]], axis=1)
        middle_first = jnp.concatenate([q[:, 1:3], q[:, 0:1], q[:, 3:4]], axis=1)
        return jnp.where(zh == 0, ends_first, middle_first).reshape(2, 2 * pair, LANES)

    def attend(q, kv, key_axis, query_axis):
        q = gather(ordered(q), query_axis).reshape(8, 2 * pair, LANES)
        kv = gather(kv.reshape(2, -1, LANES), key_axis)
        return exchange(flash(q, kv), (query_axis, "c", "zl"))

    got = spread(first, CZ)
    second, got = lax.optimization_barrier((second, got))
    got_second = spread(second, CZ)
    shared, got_second = lax.optimization_barrier((shared, got_second))
    got_shared = spread(shared, Z)

    first = merge(merge_own_body, attend(got[0], got[1:], "y", "x"), (2, 2, pair, LANES))
    second = attend(got_second[0], got_second[1:], "x", "y")
    second = merge(merge_own_body, second, (2, 2, pair, LANES))
    q, q_there = got_shared[0], flip(got_shared[0], "c")
    q = jnp.concatenate(
        [jnp.where(core == 0, q, q_there), jnp.where(core == 0, q_there, q)], axis=0
    )
    shared = merge(merge_shared_body, attend(q, got_shared[1:], "y", "x"), (2, pair, LANES))

    groups = [
        jnp.concatenate([first[z, 0], second[z, 0], first[z, 1], second[z, 1], shared[z]], axis=1)
        for z in range(2)
    ]
    for_own = jnp.where(core == 0, groups[0], groups[1])
    for_other = jnp.where(core == 0, groups[1], groups[0])
    width = out_weight.shape[1] // 2
    outs = []
    for part in range(2):
        columns = slice(part * width, (part + 1) * width)
        partial = jnp.dot(
            for_own, out_weight[:, columns], preferred_element_type=F32
        ) + jnp.dot(for_other, other_weight[:, columns], preferred_element_type=F32)
        low, high = partial[:own_rows], partial[own_rows:]
        theirs = jnp.where(zh == 0, high, low).astype(BF16)
        ours = jnp.where(zh == 0, low, high)
        projected = ours + flip(theirs, "zh", "zl").astype(F32)
        outs.append(
            (residual[:, columns].astype(F32) + gate_scale[columns] * projected).astype(BF16)
        )
    return jnp.concatenate(outs, axis=1)


def solution(mesh):
    fine = Mesh(mesh.devices.reshape(tuple(SIZES.values())), ALL)
    tokens = P(ALL, None)
    return jax.shard_map(
        on_device,
        mesh=fine,
        in_specs=(tokens, tokens, tokens, tokens, P(("zh", "c"), None), P()),
        out_specs=tokens,
        check_vma=False,
    )
```

time: 196 us -> 269 us (1.37)
  waiting for transfers between devices: 37.3 us -> 101 us
  starting transfers between devices: 78.5 us -> 61.1 us
  local copies, waits for them, and re-layouts: 3.22 us -> 19.5 us
  blocking collectives: 11.9 us -> 17.5 us
  matrix products: 6.69 us -> 11.7 us
    all_to_all x2 -> x11, waiting for transfers between devices: 0.01 us -> 76.8 us  [exchange(): return lax.all_to_all(x, axes, split_axis=0, concat_axis=0, tiled=True)]
    ppermute x34 -> x4, starting transfers between devices: 62.4 us -> 11.6 us  [flip(): return lax.ppermute(x, names, [(i, total - 1 - i) for i in range(total)])]
    all_to_all x2 -> x11, starting transfers between devices: 16 us -> 49.5 us  [exchange(): return lax.all_to_all(x, axes, split_axis=0, concat_axis=0, tiled=True)]
    ppermute x34 -> x4, waiting for transfers between devices: 37.3 us -> 23.7 us  [flip(): return lax.ppermute(x, names, [(i, total - 1 - i) for i in range(total)])]
    broadcast_in_dim x0 -> x6, local copies, waits for them, and re-layouts: none -> 8.57 us  [gather(): return exchange(jnp.broadcast_to(x[None], (SIZES[axis],) + x.shape), axis)]
    unnamed x30 -> x32, local copies, waits for them, and re-layouts: 1.42 us -> 7.99 us
    all_to_all x1, blocking collectives: 11.9 us -> 17.5 us  [exchange(): return lax.all_to_all(x, axes, split_axis=0, concat_axis=0, tiled=True)]
    dot_general x2 -> x4, matrix products: 6.69 us -> 11.7 us  [the longest x2 5.87 us: on_device(): jnp.dot(for_other, other_weight[:, columns], preferred_element_type=F32)]
  transfers between devices with their start and end apart: 36 -> 15, of which waited for: 9 -> 11; matrix products, arithmetic and copies ran while one was open for 2% -> 6% of each run, Pallas kernels for 26% -> 19%
where the time goes in v2:
time: 269 us; the launch traced here: 267 us
  waiting for transfers between devices  101 us (38%)
  starting transfers between devices  61.1 us (23%)
  Pallas kernels  54.3 us (20%)
  local copies, waits for them, and re-layouts  19.5 us (7%)
  blocking collectives  17.5 us (7%)
  matrix products  11.7 us (4%)
    all_to_all x11, waiting for transfers between devices, exchange(): return lax.all_to_all(x, axes, split_axis=0, concat_axis=0, tiled=True)  76.8 us
    all_to_all x11, starting transfers between devices, exchange(): return lax.all_to_all(x, axes, split_axis=0, concat_axis=0, tiled=True)  49.5 us
    pallas_call x3, Pallas kernels, flash(): pl.pallas_call(functools.partial(flash_body, rows), out_shape=jax.ShapeDt...  42.8 us
    ppermute x4, waiting for transfers between devices, flip(): return lax.ppermute(x, names, [(i, total - 1 - i) for i in range(total)])  23.7 us
    all_to_all x1, blocking collectives, exchange(): return lax.all_to_all(x, axes, split_axis=0, concat_axis=0, tiled=True)  17.5 us
    ppermute x4, starting transfers between devices, flip(): return lax.ppermute(x, names, [(i, total - 1 - i) for i in range(total)])  11.6 us
    pallas_call x3, Pallas kernels, merge(): pl.pallas_call(functools.partial(body, shape[-2]), out_shape=jax.ShapeDty...  8.66 us
    broadcast_in_dim x6, local copies, waits for them, and re-layouts, gather(): return exchange(jnp.broadcast_to(x[None], (SIZES[axis],) + x.shape), axis)  8.57 us
  transfers between devices with their start and end apart: 15, of which 11 were waited for; matrix products, arithmetic and copies ran while one was open for 6% of the time, Pallas kernels for 19%

profile of v2, /device:TPU:1, one launch (start us, length us, event | category | flops | bytes accessed | tf_op | source)
XLA Modules:
  0.0 267.1 jit_solution(15203112476637656734)
XLA Ops:
  2.8 17.5 %all_to_all.60 = bf16[8,3,104,128]{3,2,1,0:T(8,128)(2,1)S(1)} all-to-all(bf16[8,3,104,128]{3,2,1,0:T(8,128)(2,1)} %get-tuple-element.13), channel_id=1, replica_groups=mesh['zh'=2,'c'=2,'y'=4,'zl'=2,'x'=4] {'c','zh','zl'}, dimensions={0} | all-to-all | bytes 1277952 | tf_op jit(solution)/shard_map/all_to_all | solution.py:31
  20.3 3.9 %all-to-all-start.4 = ((bf16[8,3,104,128]{3,2,1,0:T(8,128)(2,1)}), bf16[8,3,104,128]{3,2,1,0:T(8,128)(2,1)S(1)}, u32[]{:S(2)}, u32[]{:S(2)}) async-start(bf16[8,3,104,128]{3,2,1,0:T(8,128)(2,1)} %get-tuple-element.16), calls=%async_computation.4 | async-start | bytes 1277952 | tf_op jit(solution)/shard_map/all_to_all | solution.py:31
  24.3 10.5 %all-to-all-done.4 = bf16[8,3,104,128]{3,2,1,0:T(8,128)(2,1)S(1)} async-done(((bf16[8,3,104,128]{3,2,1,0:T(8,128)(2,1)}), bf16[8,3,104,128]{3,2,1,0:T(8,128)(2,1)S(1)}, u32[]{:S(2)}, u32[]{:S(2)}) %all-to-all-start.4) | async-done | bytes 639008 | tf_op jit(solution)/shard_map/all_to_all | solution.py:31
  34.8 3.5 %all-to-all-start.8 = ((bf16[4,3,104,128]{3,2,1,0:T(8,128)(2,1)}), bf16[4,3,104,128]{3,2,1,0:T(8,128)(2,1)S(1)}, u32[]{:S(2)}, u32[]{:S(2)}) async-start(bf16[4,3,104,128]{3,2,1,0:T(8,128)(2,1)} %get-tuple-element.18), calls=%async_computation.8 | async-start | bytes 638976 | tf_op jit(solution)/shard_map/all_to_all | solution.py:31
  38.4 6.8 %all-to-all-done.8 = bf16[4,3,104,128]{3,2,1,0:T(8,128)(2,1)S(1)} async-done(((bf16[4,3,104,128]{3,2,1,0:T(8,128)(2,1)}), bf16[4,3,104,128]{3,2,1,0:T(8,128)(2,1)S(1)}, u32[]{:S(2)}, u32[]{:S(2)}) %all-to-all-start.8) | async-done | bytes 319520 | tf_op jit(solution)/shard_map/all_to_all | solution.py:31
  46.3 4.2 %all-to-all-start.5 = ((bf16[4,2,416,128]{3,2,1,0:T(8,128)(2,1)}), bf16[4,2,416,128]{3,2,1,0:T(8,128)(2,1)S(1)}, u32[]{:S(2)}, u32[]{:S(2)}) async-start(bf16[4,2,416,128]{3,2,1,0:T(8,128)(2,1)} %broadcast_in_dim.41), calls=%async_computation.5 | async-start | bytes 1703936 | tf_op jit(solution)/shard_map/all_to_all | solution.py:31
  50.5 11.5 %all-to-all-done.5 = bf16[4,2,416,128]{3,2,1,0:T(8,128)(2,1)S(1)} async-done(((bf16[4,2,416,128]{3,2,1,0:T(8,128)(2,1)}), bf16[4,2,416,128]{3,2,1,0:T(8,128)(2,1)S(1)}, u32[]{:S(2)}, u32[]{:S(2)}) %all-to-all-start.5) | async-done | bytes 852000 | tf_op jit(solution)/shard_map/all_to_all | solution.py:31
  63.1 4.0 %all-to-all-start.1 = ((bf16[4,2,416,128]{3,2,1,0:T(8,128)(2,1)}), bf16[4,2,416,128]{3,2,1,0:T(8,128)(2,1)S(1)}, u32[]{:S(2)}, u32[]{:S(2)}) async-start(bf16[4,2,416,128]{3,2,1,0:T(8,128)(2,1)} %broadcast_in_dim.18), calls=%async_computation.1 | async-start | bytes 1703936 | tf_op jit(solution)/shard_map/all_to_all | solution.py:31
  67.2 10.0 %all-to-all-done.1 = bf16[4,2,416,128]{3,2,1,0:T(8,128)(2,1)S(1)} async-done(((bf16[4,2,416,128]{3,2,1,0:T(8,128)(2,1)}), bf16[4,2,416,128]{3,2,1,0:T(8,128)(2,1)S(1)}, u32[]{:S(2)}, u32[]{:S(2)}) %all-to-all-start.1) | async-done | bytes 852000 | tf_op jit(solution)/shard_map/all_to_all | solution.py:31
  78.7 3.6 %all-to-all-start.2 = ((bf16[4,2,832,128]{3,2,1,0:T(8,128)(2,1)}), bf16[4,2,832,128]{3,2,1,0:T(8,128)(2,1)S(1)}, u32[]{:S(2)}, u32[]{:S(2)}) async-start(bf16[4,2,832,128]{3,2,1,0:T(8,128)(2,1)} %broadcast_in_dim.40), calls=%async_computation.2 | async-start | bytes 3407872 | tf_op jit(solution)/shard_map/all_to_all | solution.py:31
  82.3 4.0 %collective-permute-start = (bf16[1,4,104,128]{3,2,0,1:T(8,128)(2,1)S(1)}, bf16[1,4,104,128]{3,2,0,1:T(8,128)(2,1)S(1)}, u32[]{:S(2)}, u32[]{:S(2)}) collective-permute-start(bf16[1,4,104,128]{3,2,0,1:T(8,128)(2,1)S(1)} %slice.172), channel_id=1, source_target_pairs={{0,32},{32,0},{1,33},{33,1},{2,34},{34,2},{3,35},{35,3},{4,36},{36... | collective-permute-start | bytes 319496 | tf_op jit(solution)/shard_map/ppermute | solution.py:27
  86.3 14.2 %all-to-all-done.2.kv_ref = bf16[4,2,832,128]{3,2,1,0:T(8,128)(2,1)S(1)} async-done(((bf16[4,2,832,128]{3,2,1,0:T(8,128)(2,1)}), bf16[4,2,832,128]{3,2,1,0:T(8,128)(2,1)S(1)}, u32[]{:S(2)}, u32[]{:S(2)}) %all-to-all-start.2) | async-done | bytes 1703968 | tf_op jit(solution)/shard_map/all_to_all | solution.py:31
  101.5 3.5 %all-to-all-start.10 = ((bf16[4,2,416,128]{3,2,1,0:T(8,128)(2,1)}), bf16[4,2,416,128]{3,2,1,0:T(8,128)(2,1)S(1)}, u32[]{:S(2)}, u32[]{:S(2)}) async-start(bf16[4,2,416,128]{3,2,1,0:T(8,128)(2,1)} %broadcast_in_dim.46), calls=%async_computation.10 | async-start | bytes 1703936 | tf_op jit(solution)/shard_map/all_to_all | solution.py:31
  105.0 4.9 %collective-permute-start.1 = (bf16[640,5120]{1,0:T(8,128)(2,1)}, bf16[640,5120]{1,0:T(8,128)(2,1)}, u32[]{:S(2)}, u32[]{:S(2)}) collective-permute-start(bf16[640,5120]{1,0:T(8,128)(2,1)} %param.10), channel_id=1, source_target_pairs={{0,32},{32,0},{1,33},{33,1},{2,34},{34,2},{3,35},{35,3},{4,36},{36... | collective-permute-start | bytes 19660808 | tf_op jit(solution)/shard_map/ppermute | solution.py:27
  110.1 3.6 %all-to-all-done.10.kv_ref = bf16[4,2,416,128]{3,2,1,0:T(8,128)(2,1)S(1)} async-done(((bf16[4,2,416,128]{3,2,1,0:T(8,128)(2,1)}), bf16[4,2,416,128]{3,2,1,0:T(8,128)(2,1)S(1)}, u32[]{:S(2)}, u32[]{:S(2)}) %all-to-all-start.10) | async-done | bytes 852000 | tf_op jit(solution)/shard_map/all_to_all | solution.py:31
  114.8 3.5 %all-to-all-start.9 = ((bf16[4,2,416,128]{3,2,1,0:T(8,128)(2,1)}), bf16[4,2,416,128]{3,2,1,0:T(8,128)(2,1)S(1)}, u32[]{:S(2)}, u32[]{:S(2)}) async-start(bf16[4,2,416,128]{3,2,1,0:T(8,128)(2,1)} %broadcast_in_dim.44), calls=%async_computation.9 | async-start | bytes 1703936 | tf_op jit(solution)/shard_map/all_to_all | solution.py:31
  120.2 6.8 %all-to-all-done.9 = bf16[4,2,416,128]{3,2,1,0:T(8,128)(2,1)S(1)} async-done(((bf16[4,2,416,128]{3,2,1,0:T(8,128)(2,1)}), bf16[4,2,416,128]{3,2,1,0:T(8,128)(2,1)S(1)}, u32[]{:S(2)}, u32[]{:S(2)}) %all-to-all-start.9) | async-done | bytes 852000 | tf_op jit(solution)/shard_map/all_to_all | solution.py:31
  129.8 3.6 %all-to-all-start.6 = ((bf16[4,2,832,128]{3,2,1,0:T(8,128)(2,1)}), bf16[4,2,832,128]{3,2,1,0:T(8,128)(2,1)S(1)}, u32[]{:S(2)}, u32[]{:S(2)}) async-start(bf16[4,2,832,128]{3,2,1,0:T(8,128)(2,1)} %broadcast_in_dim.43), calls=%async_computation.6 | async-start | bytes 3407872 | tf_op jit(solution)/shard_map/all_to_all | solution.py:31
  134.5 15.7 %shard_map.65 = bf16[16,224,128]{2,1,0:T(8,128)(2,1)S(1)} custom-call(bf16[8,416,128]{2,1,0:T(8,128)(2,1)S(1)} %bitcast.61, bf16[4,2,832,128]{3,2,1,0:T(8,128)(2,1)S(1)} %all-to-all-done.2.kv_ref), custom_call_target="tpu_custom_call" | custom-call | flops 11341398016 | bytes 4194304 | tf_op jit(solution)/shard_map/pallas_call | solution.py:129
  151.2 11.9 %all-to-all-start.3 = ((bf16[16,224,128]{2,1,0:T(8,128)(2,1)}), bf16[16,224,128]{2,1,0:T(8,128)(2,1)}, u32[]{:S(2)}, u32[]{:S(2)}) async-start(bf16[16,224,128]{2,1,0:T(8,128)(2,1)} %copy-done), calls=%async_computation.3 | async-start | bytes 1835008 | tf_op jit(solution)/shard_map/all_to_all | solution.py:31
  165.4 10.5 %shard_map.69 = bf16[16,224,128]{2,1,0:T(8,128)(2,1)} custom-call(bf16[8,416,128]{2,1,0:T(8,128)(2,1)S(1)} %bitcast.62, bf16[4,2,416,128]{3,2,1,0:T(8,128)(2,1)S(1)} %copy-done.6), custom_call_target="tpu_custom_call" | custom-call | flops 5670699008 | bytes 4194304 | tf_op jit(solution)/shard_map/pallas_call | solution.py:129
  175.9 3.7 %all-to-all-done.3.x = bf16[16,224,128]{2,1,0:T(8,128)(2,1)} async-done(((bf16[16,224,128]{2,1,0:T(8,128)(2,1)}), bf16[16,224,128]{2,1,0:T(8,128)(2,1)}, u32[]{:S(2)}, u32[]{:S(2)}) %all-to-all-start.3) | async-done | bytes 917536 | tf_op jit(solution)/shard_map/all_to_all | solution.py:31
  179.5 4.2 %all-to-all-start.11 = ((bf16[16,224,128]{2,1,0:T(8,128)(2,1)}), bf16[16,224,128]{2,1,0:T(8,128)(2,1)}, u32[]{:S(2)}, u32[]{:S(2)}) async-start(bf16[16,224,128]{2,1,0:T(8,128)(2,1)} %shard_map.69), calls=%async_computation.11 | async-start | bytes 1835008 | tf_op jit(solution)/shard_map/all_to_all | solution.py:31
  183.8 16.6 %shard_map.67 = bf16[16,224,128]{2,1,0:T(8,128)(2,1)} custom-call(bf16[8,416,128]{2,1,0:T(8,128)(2,1)S(1)} %bitcast.60, bf16[4,2,832,128]{3,2,1,0:T(8,128)(2,1)S(1)} %all-to-all-done.6.kv_ref), custom_call_target="tpu_custom_call" | custom-call | flops 11341398016 | bytes 4194304 | tf_op jit(solution)/shard_map/pallas_call | solution.py:129
  200.4 3.7 %all-to-all-start.7 = ((bf16[16,224,128]{2,1,0:T(8,128)(2,1)}), bf16[16,224,128]{2,1,0:T(8,128)(2,1)S(1)}, u32[]{:S(2)}, u32[]{:S(2)}) async-start(bf16[16,224,128]{2,1,0:T(8,128)(2,1)} %shard_map.67), calls=%async_computation.7 | async-start | bytes 1835008 | tf_op jit(solution)/shard_map/all_to_all | solution.py:31
  210.8 9.6 %all-to-all-done.7.x = bf16[16,224,128]{2,1,0:T(8,128)(2,1)S(1)} async-done(((bf16[16,224,128]{2,1,0:T(8,128)(2,1)}), bf16[16,224,128]{2,1,0:T(8,128)(2,1)S(1)}, u32[]{:S(2)}, u32[]{:S(2)}) %all-to-all-start.7) | async-done | bytes 917536 | tf_op jit(solution)/shard_map/all_to_all | solution.py:31
  226.9 2.9 %fusion.2 = f32[208,2560]{1,0:T(8,128)S(1)} fusion(bf16[640,5120]{1,0:T(8,128)(2,1)} %param.10, bf16[208,640]{1,0:T(8,128)(2,1)S(1)} %get-tuple-element.38, bf16[208,640]{1,0:T(8,128)(2,1)S(1)} %get-tuple-element.37, pred[]{:T(512)S(6)} %eq.5), kind=kOutput, calls=%fused_computation.4 | convolution fusion | flops 681707520 | bytes 5939201 | tf_op jit(solution)/shard_map/dot_general | solution.py:218
  229.8 2.9 %fusion.4 = f32[208,2560]{1,0:T(8,128)S(1)} fusion(bf16[640,5120]{1,0:T(8,128)(2,1)} %param.10, bf16[208,640]{1,0:T(8,128)(2,1)S(1)} %get-tuple-element.38, bf16[208,640]{1,0:T(8,128)(2,1)S(1)} %get-tuple-element.37, pred[]{:T(512)S(6)} %eq.5), kind=kOutput, calls=%fused_computation.6 | convolution fusion | flops 681707520 | bytes 5939201 | tf_op jit(solution)/shard_map/dot_general | solution.py:218
  232.8 2.9 %convolution_add_fusion.1 = f32[208,2560]{1,0:T(8,128)S(1)} fusion(f32[208,2560]{1,0:T(8,128)S(1)} %fusion.4, bf16[640,5120]{1,0:T(8,128)(2,1)} %collective-permute-done.1, bf16[208,640]{1,0:T(8,128)(2,1)S(1)} %get-tuple-element.37, bf16[208,640]{1,0:T(8,128)(2,1)S(1)} %get-tuple-element.38, pred[]{:T(512)S(6)} %eq.5), kind=kOutput, calls=%fused_computation.1 | convolution fusion | flops 682240000 | bytes 8069121 | tf_op jit(solution)/shard_map/dot_general | solution.py:220
  235.8 2.9 %convolution_add_fusion = f32[208,2560]{1,0:T(8,128)S(1)} fusion(f32[208,2560]{1,0:T(8,128)S(1)} %fusion.2, bf16[640,5120]{1,0:T(8,128)(2,1)} %collective-permute-done.1, bf16[208,640]{1,0:T(8,128)(2,1)S(1)} %get-tuple-element.37, bf16[208,640]{1,0:T(8,128)(2,1)S(1)} %get-tuple-element.38, pred[]{:T(512)S(6)} %eq.5), kind=kOutput, calls=%fused_computation | convolution fusion | flops 682240000 | bytes 8069121 | tf_op jit(solution)/shard_map/dot_general | solution.py:220
  241.7 12.3 %collective-permute-done.3 = bf16[104,2560]{1,0:T(8,128)(2,1)S(1)} collective-permute-done((bf16[104,2560]{1,0:T(8,128)(2,1)S(1)}, bf16[104,2560]{1,0:T(8,128)(2,1)S(1)}, u32[]{:S(2)}, u32[]{:S(2)}) %collective-permute-start.3) | collective-permute-done | bytes 532512 | tf_op jit(solution)/shard_map/ppermute | solution.py:27
  254.0 11.4 %collective-permute-done.2 = bf16[104,2560]{1,0:T(8,128)(2,1)S(1)} collective-permute-done((bf16[104,2560]{1,0:T(8,128)(2,1)S(1)}, bf16[104,2560]{1,0:T(8,128)(2,1)S(1)}, u32[]{:S(2)}, u32[]{:S(2)}) %collective-permute-start.2) | collective-permute-done | bytes 532512 | tf_op jit(solution)/shard_map/ppermute | solution.py:27
  (75 shorter events, 35.7 us)
Async XLA Ops:
  20.3 14.5 %all-to-all-start.4 = ((bf16[8,3,104,128]{3,2,1,0:T(8,128)(2,1)}), bf16[8,3,104,128]{3,2,1,0:T(8,128)(2,1)S(1)}, u32[]{:S(2)}, u32[]{:S(2)}) async-start(bf16[8,3,104,128]{3,2,1,0:T(8,128)(2,1)} %get-tuple-element.16), calls=%async_computation.4 | async-start | bytes 1277952 | tf_op jit(solution)/shard_map/all_to_all | solution.py:31
  34.8 11.5 %copy-start.10 = (bf16[8,3,104,128]{3,2,1,0:T(8,128)(2,1)}, bf16[8,3,104,128]{3,2,1,0:T(8,128)(2,1)S(1)}, u32[]{:S(2)}) copy-start(bf16[8,3,104,128]{3,2,1,0:T(8,128)(2,1)S(1)} %all-to-all-done.4) | copy-start | bytes 1916932
  34.8 10.5 %all-to-all-start.8 = ((bf16[4,3,104,128]{3,2,1,0:T(8,128)(2,1)}), bf16[4,3,104,128]{3,2,1,0:T(8,128)(2,1)S(1)}, u32[]{:S(2)}, u32[]{:S(2)}) async-start(bf16[4,3,104,128]{3,2,1,0:T(8,128)(2,1)} %get-tuple-element.18), calls=%async_computation.8 | async-start | bytes 638976 | tf_op jit(solution)/shard_map/all_to_all | solution.py:31
  46.3 15.7 %all-to-all-start.5 = ((bf16[4,2,416,128]{3,2,1,0:T(8,128)(2,1)}), bf16[4,2,416,128]{3,2,1,0:T(8,128)(2,1)S(1)}, u32[]{:S(2)}, u32[]{:S(2)}) async-start(bf16[4,2,416,128]{3,2,1,0:T(8,128)(2,1)} %broadcast_in_dim.41), calls=%async_computation.5 | async-start | bytes 1703936 | tf_op jit(solution)/shard_map/all_to_all | solution.py:31
  62.0 5.2 %copy-start.1 = (bf16[4,2,416,128]{3,2,1,0:T(8,128)(2,1)}, bf16[4,2,416,128]{3,2,1,0:T(8,128)(2,1)S(1)}, u32[]{:S(2)}) copy-start(bf16[4,2,416,128]{3,2,1,0:T(8,128)(2,1)S(1)} %all-to-all-done.5) | copy-start | bytes 2555908
  63.1 14.1 %all-to-all-start.1 = ((bf16[4,2,416,128]{3,2,1,0:T(8,128)(2,1)}), bf16[4,2,416,128]{3,2,1,0:T(8,128)(2,1)S(1)}, u32[]{:S(2)}, u32[]{:S(2)}) async-start(bf16[4,2,416,128]{3,2,1,0:T(8,128)(2,1)} %broadcast_in_dim.18), calls=%async_computation.1 | async-start | bytes 1703936 | tf_op jit(solution)/shard_map/all_to_all | solution.py:31
  77.2 1.5 copy-start.3
  78.7 21.8 %all-to-all-start.2 = ((bf16[4,2,832,128]{3,2,1,0:T(8,128)(2,1)}), bf16[4,2,832,128]{3,2,1,0:T(8,128)(2,1)S(1)}, u32[]{:S(2)}, u32[]{:S(2)}) async-start(bf16[4,2,832,128]{3,2,1,0:T(8,128)(2,1)} %broadcast_in_dim.40), calls=%async_computation.2 | async-start | bytes 3407872 | tf_op jit(solution)/shard_map/all_to_all | solution.py:31
  82.3 27.6 %collective-permute-start = (bf16[1,4,104,128]{3,2,0,1:T(8,128)(2,1)S(1)}, bf16[1,4,104,128]{3,2,0,1:T(8,128)(2,1)S(1)}, u32[]{:S(2)}, u32[]{:S(2)}) collective-permute-start(bf16[1,4,104,128]{3,2,0,1:T(8,128)(2,1)S(1)} %slice.172), channel_id=1, source_target_pairs={{0,32},{32,0},{1,33},{33,1},{2,34},{34,2},{3,35},{35,3},{4,36},{36... | collective-permute-start | bytes 319496 | tf_op jit(solution)/shard_map/ppermute | solution.py:27
  101.5 12.2 %all-to-all-start.10 = ((bf16[4,2,416,128]{3,2,1,0:T(8,128)(2,1)}), bf16[4,2,416,128]{3,2,1,0:T(8,128)(2,1)S(1)}, u32[]{:S(2)}, u32[]{:S(2)}) async-start(bf16[4,2,416,128]{3,2,1,0:T(8,128)(2,1)} %broadcast_in_dim.46), calls=%async_computation.10 | async-start | bytes 1703936 | tf_op jit(solution)/shard_map/all_to_all | solution.py:31
  105.0 127.7 %collective-permute-start.1 = (bf16[640,5120]{1,0:T(8,128)(2,1)}, bf16[640,5120]{1,0:T(8,128)(2,1)}, u32[]{:S(2)}, u32[]{:S(2)}) collective-permute-start(bf16[640,5120]{1,0:T(8,128)(2,1)} %param.10), channel_id=1, source_target_pairs={{0,32},{32,0},{1,33},{33,1},{2,34},{34,2},{3,35},{35,3},{4,36},{36... | collective-permute-start | bytes 19660808 | tf_op jit(solution)/shard_map/ppermute | solution.py:27
  113.7 6.5 %copy-start.5 = (bf16[4,2,416,128]{3,2,1,0:T(8,128)(2,1)}, bf16[4,2,416,128]{3,2,1,0:T(8,128)(2,1)S(1)}, u32[]{:S(2)}) copy-start(bf16[4,2,416,128]{3,2,1,0:T(8,128)(2,1)S(1)} %all-to-all-done.10.kv_ref) | copy-start | bytes 2555908
  114.8 12.2 %all-to-all-start.9 = ((bf16[4,2,416,128]{3,2,1,0:T(8,128)(2,1)}), bf16[4,2,416,128]{3,2,1,0:T(8,128)(2,1)S(1)}, u32[]{:S(2)}, u32[]{:S(2)}) async-start(bf16[4,2,416,128]{3,2,1,0:T(8,128)(2,1)} %broadcast_in_dim.44), calls=%async_computation.9 | async-start | bytes 1703936 | tf_op jit(solution)/shard_map/all_to_all | solution.py:31
  127.0 2.8 %copy-start.7 = (bf16[4,2,416,128]{3,2,1,0:T(8,128)(2,1)}, bf16[4,2,416,128]{3,2,1,0:T(8,128)(2,1)S(1)}, u32[]{:S(2)}) copy-start(bf16[4,2,416,128]{3,2,1,0:T(8,128)(2,1)S(1)} %all-to-all-done.9) | copy-start | bytes 2555908
  129.8 21.4 %all-to-all-start.6 = ((bf16[4,2,832,128]{3,2,1,0:T(8,128)(2,1)}), bf16[4,2,832,128]{3,2,1,0:T(8,128)(2,1)S(1)}, u32[]{:S(2)}, u32[]{:S(2)}) async-start(bf16[4,2,832,128]{3,2,1,0:T(8,128)(2,1)} %broadcast_in_dim.43), calls=%async_computation.6 | async-start | bytes 3407872 | tf_op jit(solution)/shard_map/all_to_all | solution.py:31
  133.4 1.2 copy-start.4
  150.2 0.9 copy-start
  151.2 28.4 %all-to-all-start.3 = ((bf16[16,224,128]{2,1,0:T(8,128)(2,1)}), bf16[16,224,128]{2,1,0:T(8,128)(2,1)}, u32[]{:S(2)}, u32[]{:S(2)}) async-start(bf16[16,224,128]{2,1,0:T(8,128)(2,1)} %copy-done), calls=%async_computation.3 | async-start | bytes 1835008 | tf_op jit(solution)/shard_map/all_to_all | solution.py:31
  163.1 1.2 copy-start.6
  164.2 1.2 copy-start.8
  165.4 18.4 %copy-start.2 = (bf16[4,2,416,128]{3,2,1,0:T(8,128)(2,1)S(1)}, bf16[4,2,416,128]{3,2,1,0:T(8,128)(2,1)}, u32[]{:S(2)}) copy-start(bf16[4,2,416,128]{3,2,1,0:T(8,128)(2,1)} %copy-done.1) | copy-start | bytes 2555908
  179.5 20.9 %all-to-all-start.11 = ((bf16[16,224,128]{2,1,0:T(8,128)(2,1)}), bf16[16,224,128]{2,1,0:T(8,128)(2,1)}, u32[]{:S(2)}, u32[]{:S(2)}) async-start(bf16[16,224,128]{2,1,0:T(8,128)(2,1)} %shard_map.69), calls=%async_computation.11 | async-start | bytes 1835008 | tf_op jit(solution)/shard_map/all_to_all | solution.py:31
  200.4 20.1 %all-to-all-start.7 = ((bf16[16,224,128]{2,1,0:T(8,128)(2,1)}), bf16[16,224,128]{2,1,0:T(8,128)(2,1)S(1)}, u32[]{:S(2)}, u32[]{:S(2)}) async-start(bf16[16,224,128]{2,1,0:T(8,128)(2,1)} %shard_map.67), calls=%async_computation.7 | async-start | bytes 1835008 | tf_op jit(solution)/shard_map/all_to_all | solution.py:31
  207.0 18.1 %copy-start.12 = (bf16[2,2,208,128]{3,2,1,0:T(8,128)(2,1)S(1)}, bf16[2,2,208,128]{3,2,1,0:T(8,128)(2,1)}, u32[]{:S(2)}) copy-start(bf16[2,2,208,128]{3,2,1,0:T(8,128)(2,1)} %shard_map.66) | copy-start | bytes 638980
  220.5 0.9 copy-start.9
  235.8 5.8 %copy-start.13 = (f32[5120]{0:T(1024)S(1)}, f32[5120]{0:T(1024)}, u32[]{:S(2)}) copy-start(f32[5120]{0:T(1024)} %param.11) | copy-start | bytes 61444
  238.8 26.6 %copy-start.11 = (bf16[104,5120]{1,0:T(8,128)(2,1)S(1)}, bf16[104,5120]{1,0:T(8,128)(2,1)}, u32[]{:S(2)}) copy-start(bf16[104,5120]{1,0:T(8,128)(2,1)} %param.9) | copy-start | bytes 3194884
  238.9 15.1 %collective-permute-start.3 = (bf16[104,2560]{1,0:T(8,128)(2,1)S(1)}, bf16[104,2560]{1,0:T(8,128)(2,1)S(1)}, u32[]{:S(2)}, u32[]{:S(2)}) collective-permute-start(bf16[104,2560]{1,0:T(8,128)(2,1)S(1)} %select_convert_fusion), channel_id=1, source_target_pairs={{0,68},{4,64},{64,4},{68,0},{1,69},{5,65},{65,5},{69,1},{2,70},{6,... | collective-permute-start | bytes 1597448 | tf_op jit(solution)/shard_map/ppermute | solution.py:27
  239.9 25.5 %collective-permute-start.2 = (bf16[104,2560]{1,0:T(8,128)(2,1)S(1)}, bf16[104,2560]{1,0:T(8,128)(2,1)S(1)}, u32[]{:S(2)}, u32[]{:S(2)}) collective-permute-start(bf16[104,2560]{1,0:T(8,128)(2,1)S(1)} %select_convert_fusion.1), channel_id=1, source_target_pairs={{0,68},{4,64},{64,4},{68,0},{1,69},{5,65},{65,5},{69,1},{2,70},{6,... | collective-permute-start | bytes 1597448 | tf_op jit(solution)/shard_map/ppermute | solution.py:27

commit v3 on v2

v3 whole, which is shorter than its diff:
```python
import functools

import jax
import jax.numpy as jnp
from jax import lax
from jax.experimental import pallas as pl
from jax.experimental.pallas import tpu as pltpu
from jax.sharding import Mesh
from jax.sharding import PartitionSpec as P

HEAD_DIM = 128
LANES = 128
SCALE = HEAD_DIM**-0.5 * 1.4426950408889634
ALL = ("zh", "c", "y", "zl", "x")
SIZES = {"zh": 2, "c": 2, "y": 4, "zl": 2, "x": 4}
Z = ("zh", "zl")
CZ = ("c", "zh", "zl")
KEY_TILE = 256
LEVEL_ROWS = 16
F32 = jnp.float32
BF16 = jnp.bfloat16
NT = (((1,), (1,)), ((), ()))


def flip(x, *names):
    total = 2 ** len(names)
    return lax.ppermute(x, names, [(i, total - 1 - i) for i in range(total)])


def exchange(x, axes):
    return lax.all_to_all(x, axes, split_axis=0, concat_axis=0, tiled=True)


def shift(x, axis, by):
    n = SIZES[axis]
    return lax.ppermute(x, axis, [(i, (i + by) % n) for i in range(n)])


def gather(x, axis):
    left, right = shift(x, axis, 1), shift(x, axis, -1)
    return [x, left, right, shift(left[0], axis, 1), shift(right[1], axis, -1)]


def cut_body(q, k, v, shared, first, second):
    for i, x in enumerate((q, k, v)):
        for z in range(4):
            for out, heads in ((shared, (4,)), (first, (0, 1)), (second, (2, 3))):
                for c, head in enumerate(heads):
                    lanes = slice((5 * z + head) * LANES, (5 * z + head + 1) * LANES)
                    out[4 * c + z, i] = x[:, lanes]


def cut(q, k, v):
    rows = q.shape[0]
    return pl.pallas_call(
        cut_body,
        out_shape=[jax.ShapeDtypeStruct((n, 3, rows, LANES), BF16) for n in (4, 8, 8)],
    )(q, k, v)


def eye(rows):
    return lax.broadcasted_iota(jnp.int32, (rows, LANES), 0) == lax.broadcasted_iota(
        jnp.int32, (rows, LANES), 1
    )


def write_levels(out, at, level):
    rows = level.shape[0]
    lines = []
    for start in range(0, rows, LANES):
        piece = level[start : start + LANES]
        lines.append(jnp.sum(jnp.where(eye(piece.shape[0]), piece, 0.0), axis=0, keepdims=True))
    line = jnp.concatenate(lines, axis=0)
    high = line.astype(BF16).astype(F32)
    middle = (line - high).astype(BF16).astype(F32)
    low = line - high - middle
    spare = jnp.zeros((LEVEL_ROWS - 3 * len(lines), LANES), F32)
    out[at, rows:, :] = jnp.concatenate([high, middle, low, spare], axis=0).astype(BF16)


def read_levels(block, rows):
    n = -(-rows // LANES)
    parts = block[rows:, :].astype(F32)
    return parts[:n] + parts[n : 2 * n] + parts[2 * n : 3 * n]


def flash_body(rows, query_axis, parts, *refs):
    q_own, q_left, q_right, *q_far = refs[:5]
    kv_own, kv_left, kv_right, *kv_far = refs[5:10]
    out, queries, keys, values = refs[10:]
    me = lax.axis_index(query_axis)
    values[:, HEAD_DIM:] = jnp.ones((values.shape[0], LANES), BF16)
    half_rows = 2 * rows
    first_key = 0
    for part, key_rows in enumerate(parts):
        these = slice(first_key, first_key + key_rows)
        first_key += key_rows
        for i, ref in enumerate((kv_own, kv_left, kv_right)):
            to = slice(i * key_rows, (i + 1) * key_rows)
            keys[to, :] = ref[0, these, :]
            values[to, :HEAD_DIM] = ref[1, these, :]
        to = slice(3 * key_rows, 4 * key_rows)
        keys[to, :] = kv_far[0][these, :]
        values[to, :HEAD_DIM] = kv_far[1][these, :]
        for half in range(2):
            for place, ref in ((0, q_own), (1, q_right), (3, q_left)):
                if len(parts) == 1:
                    queries[2 * place + half] = ref[half]
                else:
                    queries[2 * place + half] = ref[part, half * half_rows : (half + 1) * half_rows, :]
            if len(parts) == 1:
                queries[4 + half] = q_far[half][...]
            else:
                queries[4 + half] = q_far[part][half * half_rows : (half + 1) * half_rows, :]

        def block(i, _):
            q = queries[i]
            largest = total = None
            for start in range(0, 4 * key_rows, KEY_TILE):
                tile = pl.ds(start, min(KEY_TILE, 4 * key_rows - start))
                scores = lax.dot_general(q, keys[tile, :], NT, preferred_element_type=F32)
                new = jnp.max(scores, axis=1, keepdims=True)
                if total is not None:
                    new = jnp.maximum(largest, new)
                weights = jnp.exp2((scores - new) * SCALE).astype(BF16)
                update = jnp.dot(weights, values[tile, :], preferred_element_type=F32)
                if total is None:
                    total = update
                else:
                    total = total * jnp.exp2((largest - new) * SCALE) + update
                largest = new
            sums = total[:, HEAD_DIM:]
            result = (total[:, :HEAD_DIM] / sums).astype(BF16)
            level = largest * SCALE + jnp.log2(sums)
            place = lax.rem(me + lax.div(i, 2), 4)
            for half in range(2):
                at = 4 * place + 2 * lax.rem(i, 2) + half
                here = slice(half * rows, (half + 1) * rows)
                out[at, part, :rows, :] = result[here]
                write_levels(out.at[at], part, level[here])
            return 0

        lax.fori_loop(0, 8, block, 0)


def flash(queries, kvs, rows, query_axis, parts):
    pairs = 16 * rows * 4 * sum(parts)
    return pl.pallas_call(
        functools.partial(flash_body, rows, query_axis, parts),
        out_shape=jax.ShapeDtypeStruct((16, len(parts), rows + LEVEL_ROWS, LANES), BF16),
        scratch_shapes=[
            pltpu.VMEM((8, 2 * rows, HEAD_DIM), BF16),
            pltpu.VMEM((4 * max(parts), HEAD_DIM), BF16),
            pltpu.VMEM((4 * max(parts), 2 * HEAD_DIM), BF16),
        ],
        compiler_params=pltpu.CompilerParams(vmem_limit_bytes=40 << 20),
        cost_estimate=pl.CostEstimate(
            flops=8 * pairs * HEAD_DIM, bytes_accessed=4 << 20, transcendentals=pairs
        ),
    )(*queries, *kvs)


def merge_blocks(blocks, rows):
    levels = [read_levels(b, rows) for b in blocks]
    top = functools.reduce(jnp.maximum, levels)
    shares = [jnp.exp2(v - top) for v in levels]
    whole = functools.reduce(jnp.add, shares)
    shares = [share / whole for share in shares]
    pieces = []
    for i, start in enumerate(range(0, rows, LANES)):
        here = min(LANES, rows - start)
        total = 0.0
        for share, b in zip(shares, blocks):
            wide = jnp.broadcast_to(share[i : i + 1, :here], (here, here))
            diagonal = jnp.where(eye(here)[:, :here], wide, 0.0).astype(BF16)
            total = total + jnp.dot(
                diagonal, b[start : start + here, :], preferred_element_type=F32
            )
        pieces.append(total.astype(BF16))
    return jnp.concatenate(pieces, axis=0)


def merge_body(rows, x, out):
    for z in range(2):
        for c in range(2):
            value = merge_blocks([x[4 * i + 2 * c + z, 0] for i in range(4)], rows)
            out[z, :, c * LANES : (c + 1) * LANES] = value
        if x.shape[1] > 1:
            both = [x[4 * i + 2 * c + z, 1] for i in range(4) for c in range(2)]
            out[z, :, 2 * LANES :] = merge_blocks(both, rows)


def merge(x):
    rows, heads = x.shape[2] - LEVEL_ROWS, x.shape[1] + 1
    return pl.pallas_call(
        functools.partial(merge_body, rows),
        out_shape=jax.ShapeDtypeStruct((2, rows, heads * LANES), BF16),
    )(x)


def on_device(query_in, key_in, value_in, residual, out_weight, gate_scale):
    own_rows = query_in.shape[0]
    pair = 2 * own_rows
    other_weight = flip(out_weight, "c")
    zh, core = lax.axis_index("zh"), lax.axis_index("c")

    shared, first, second = cut(query_in, key_in, value_in)

    def spread(x, axes):
        got = exchange(x, axes).transpose(1, 0, 2, 3)
        return got.reshape(3, -1, 4, own_rows, LANES)

    def ordered(q):
        ends_first = jnp.concatenate([q[:, 0:1], q[:, 3:4], q[:, 1:3]], axis=1)
        middle_first = jnp.concatenate([q[:, 1:3], q[:, 0:1], q[:, 3:4]], axis=1)
        return jnp.where(zh == 0, ends_first, middle_first).reshape(2, 2 * pair, LANES)

    def attend(q, kv, parts, key_axis, query_axis):
        out = flash(gather(q, query_axis), gather(kv, key_axis), pair, query_axis, parts)
        return merge(exchange(out, (query_axis, "c", "zl")))

    got = spread(first, CZ)
    second, shared, got = lax.optimization_barrier((second, shared, got))
    got_second = spread(second, CZ)
    shared, got_second = lax.optimization_barrier((shared, got_second))
    got_shared = spread(shared, Z)

    rows = 8 * own_rows
    first = attend(ordered(got[0]), got[1:].reshape(2, rows, LANES), (rows,), "y", "x")
    q_here, q_there = got_shared[0], flip(got_shared[0], "c")
    q_shared = jnp.concatenate(
        [jnp.where(core == 0, q_here, q_there), jnp.where(core == 0, q_there, q_here)], axis=0
    )
    q = jnp.stack([ordered(x).reshape(rows, LANES) for x in (got_second[0], q_shared)])
    kv = jnp.concatenate(
        [x[1:].reshape(2, -1, LANES) for x in (got_second, got_shared)], axis=1
    )
    second = attend(q, kv, (rows, rows // 2), "x", "y")

    cut_at = first.shape[2]
    width = out_weight.shape[1] // 2
    outs = []
    for part in range(2):
        columns = slice(part * width, (part + 1) * width)
        partial = 0.0
        for x, inner in ((first, slice(0, cut_at)), (second, slice(cut_at, None))):
            for_own = jnp.where(core == 0, x[0], x[1])
            for_other = jnp.where(core == 0, x[1], x[0])
            for side, weight in ((for_own, out_weight), (for_other, other_weight)):
                partial += jnp.dot(side, weight[inner, columns], preferred_element_type=F32)
        low, high = partial[:own_rows], partial[own_rows:]
        theirs = jnp.where(zh == 0, high, low).astype(BF16)
        ours = jnp.where(zh == 0, low, high)
        projected = ours + flip(theirs, "zh", "zl").astype(F32)
        outs.append(
            (residual[:, columns].astype(F32) + gate_scale[columns] * projected).astype(BF16)
        )
    return jnp.concatenate(outs, axis=1)


def solution(mesh):
    fine = Mesh(mesh.devices.reshape(tuple(SIZES.values())), ALL)
    tokens = P(ALL, None)
    return jax.shard_map(
        on_device,
        mesh=fine,
        in_specs=(tokens, tokens, tokens, tokens, P(("zh", "c"), None), P()),
        out_specs=tokens,
        check_vma=False,
    )
```

time: 269 us -> 223 us (0.83)
  blocking collectives: 17.5 us -> 0 us
  waiting for transfers between devices: 101 us -> 86 us
  local copies, waits for them, and re-layouts: 19.5 us -> 7.89 us
  starting transfers between devices: 61.1 us -> 53.8 us
  matrix products: 11.7 us -> 18.5 us
    all_to_all x11 -> x5, waiting for transfers between devices: 76.8 us -> 34.5 us  [exchange(): return lax.all_to_all(x, axes, split_axis=0, concat_axis=0, tiled=True)]
    ppermute x0 -> x16, waiting for transfers between devices: none -> 28.7 us  [shift(): return lax.ppermute(x, axis, [(i, (i + by) % n) for i in range(n)])]
    all_to_all x11 -> x5, starting transfers between devices: 49.5 us -> 27.5 us  [exchange(): return lax.all_to_all(x, axes, split_axis=0, concat_axis=0, tiled=True)]
    ppermute x0 -> x16, starting transfers between devices: none -> 20.5 us  [shift(): return lax.ppermute(x, axis, [(i, (i + by) % n) for i in range(n)])]
    all_to_all x1 -> x0, blocking collectives: 17.5 us -> none  [exchange(): return lax.all_to_all(x, axes, split_axis=0, concat_axis=0, tiled=True)]
    broadcast_in_dim x6 -> x0, local copies, waits for them, and re-layouts: 8.57 us -> none  [gather(): return exchange(jnp.broadcast_to(x[None], (SIZES[axis],) + x.shape), axis)]
    dot_general x4 -> x8, matrix products: 11.7 us -> 18.5 us  [on_device(): partial += jnp.dot(side, weight[inner, columns], preferred_element_type=F32)]
    ppermute x4, starting transfers between devices: 11.6 us -> 5.73 us  [flip(): return lax.ppermute(x, names, [(i, total - 1 - i) for i in range(total)])]
  transfers between devices with their start and end apart: 15 -> 25, of which waited for: 11 -> 11; matrix products, arithmetic and copies ran while one was open for 6% -> 5% of each run, Pallas kernels for 19% -> 23%
where the time goes in v3:
time: 223 us; the launch traced here: 222 us
  waiting for transfers between devices  86 us (39%)
  starting transfers between devices  53.8 us (24%)
  Pallas kernels  53.6 us (24%)
  matrix products  18.5 us (8%)
  local copies, waits for them, and re-layouts  7.89 us (4%)
    pallas_call x2, Pallas kernels, flash(): pl.pallas_call(functools.partial(flash_body, rows, query_axis, parts), ou...  45.4 us
    all_to_all x5, waiting for transfers between devices, exchange(): return lax.all_to_all(x, axes, split_axis=0, concat_axis=0, tiled=True)  34.5 us
    ppermute x16, waiting for transfers between devices, shift(): return lax.ppermute(x, axis, [(i, (i + by) % n) for i in range(n)])  28.7 us
    all_to_all x5, starting transfers between devices, exchange(): return lax.all_to_all(x, axes, split_axis=0, concat_axis=0, tiled=True)  27.5 us
    ppermute x4, waiting for transfers between devices, flip(): return lax.ppermute(x, names, [(i, total - 1 - i) for i in range(total)])  22.8 us
    ppermute x16, starting transfers between devices, shift(): return lax.ppermute(x, axis, [(i, (i + by) % n) for i in range(n)])  20.5 us
    dot_general x8, matrix products, on_device(): partial += jnp.dot(side, weight[inner, columns], preferred_element_type=F32)  18.5 us
    ppermute x4, starting transfers between devices, flip(): return lax.ppermute(x, names, [(i, total - 1 - i) for i in range(total)])  5.73 us
  transfers between devices with their start and end apart: 25, of which 11 were waited for; matrix products, arithmetic and copies ran while one was open for 5% of the time, Pallas kernels for 23%

profile of v3, /device:TPU:1, one launch (start us, length us, event | category | flops | bytes accessed | tf_op | source)
XLA Modules:
  0.0 222.2 jit_solution(4334278917152254904)
XLA Ops:
  0.0 2.8 %shard_map.64 = (bf16[4,3,104,128]{3,2,1,0:T(8,128)(2,1)}, bf16[8,3,104,128]{3,2,1,0:T(8,128)(2,1)}, bf16[8,3,104,128]{3,2,1,0:T(8,128)(2,1)}) custom-call(bf16[104,2560]{1,0:T(8,128)(2,1)} %q.1, bf16[104,2560]{1,0:T(8,128)(2,1)} %k.1, bf16[104,2560]{1,0:T(8,128)(2,1)} %v.1), custom_call_target="tpu_custom_call" | custom-call | tf_op jit(solution)/shard_map/pallas_call | solution.py:55
  2.8 6.8 %all-to-all-start = ((bf16[8,3,104,128]{3,2,1,0:T(8,128)(2,1)}), bf16[8,3,104,128]{3,2,1,0:T(8,128)(2,1)S(1)}, u32[]{:S(2)}, u32[]{:S(2)}) async-start(bf16[8,3,104,128]{3,2,1,0:T(8,128)(2,1)} %get-tuple-element.15), calls=%async_computation | async-start | bytes 1277952 | tf_op jit(solution)/shard_map/all_to_all | solution.py:31
  9.6 10.6 %all-to-all-done = bf16[8,3,104,128]{3,2,1,0:T(8,128)(2,1)S(1)} async-done(((bf16[8,3,104,128]{3,2,1,0:T(8,128)(2,1)}), bf16[8,3,104,128]{3,2,1,0:T(8,128)(2,1)S(1)}, u32[]{:S(2)}, u32[]{:S(2)}) %all-to-all-start) | async-done | bytes 639008 | tf_op jit(solution)/shard_map/all_to_all | solution.py:31
  20.2 3.8 %all-to-all-start.2 = ((bf16[8,3,104,128]{3,2,1,0:T(8,128)(2,1)}), bf16[8,3,104,128]{3,2,1,0:T(8,128)(2,1)S(1)}, u32[]{:S(2)}, u32[]{:S(2)}) async-start(bf16[8,3,104,128]{3,2,1,0:T(8,128)(2,1)} %get-tuple-element.18), calls=%async_computation.2 | async-start | bytes 1277952 | tf_op jit(solution)/shard_map/all_to_all | solution.py:31
  24.1 2.8 %collective-permute-start.5 = (bf16[2,832,128]{2,1,0:T(8,128)(2,1)S(1)}, bf16[2,832,128]{2,1,0:T(8,128)(2,1)S(1)}, u32[]{:S(2)}, u32[]{:S(2)}) collective-permute-start(bf16[2,832,128]{2,1,0:T(8,128)(2,1)S(1)} %bitcast.53), channel_id=1, source_target_pairs={{0,24},{8,0},{16,8},{24,16},{1,25},{9,1},{17,9},{25,17},{2,26},{10... | collective-permute-start | bytes 1277960 | tf_op jit(solution)/shard_map/ppermute | solution.py:36
  27.1 9.0 %collective-permute-done.5.refs_7_ = bf16[2,832,128]{2,1,0:T(8,128)(2,1)S(1)} collective-permute-done((bf16[2,832,128]{2,1,0:T(8,128)(2,1)S(1)}, bf16[2,832,128]{2,1,0:T(8,128)(2,1)S(1)}, u32[]{:S(2)}, u32[]{:S(2)}) %collective-permute-start.5) | collective-permute-done | bytes 426016 | tf_op jit(solution)/shard_map/ppermute | solution.py:36
  36.8 3.4 %collective-permute-start.7 = (bf16[832,128]{1,0:T(8,128)(2,1)}, bf16[832,128]{1,0:T(8,128)(2,1)}, u32[]{:S(2)}, u32[]{:S(2)}) collective-permute-start(bf16[832,128]{1,0:T(8,128)(2,1)} %slice_bitcast_fusion.5), channel_id=1, source_target_pairs={{0,24},{8,0},{16,8},{24,16},{1,25},{9,1},{17,9},{25,17},{2,26},{10... | collective-permute-start | bytes 638984 | tf_op jit(solution)/shard_map/ppermute | solution.py:36
  40.2 3.8 %all-to-all-start.3 = ((bf16[4,3,104,128]{3,2,1,0:T(8,128)(2,1)}), bf16[4,3,104,128]{3,2,1,0:T(8,128)(2,1)S(1)}, u32[]{:S(2)}, u32[]{:S(2)}) async-start(bf16[4,3,104,128]{3,2,1,0:T(8,128)(2,1)} %get-tuple-element.20), calls=%async_computation.3 | async-start | bytes 638976 | tf_op jit(solution)/shard_map/all_to_all | solution.py:31
  44.2 2.5 %collective-permute-start.1 = (bf16[2,416,128]{2,1,0:T(8,128)(2,1)S(1)}, bf16[2,416,128]{2,1,0:T(8,128)(2,1)S(1)}, u32[]{:S(2)}, u32[]{:S(2)}) collective-permute-start(bf16[2,416,128]{2,1,0:T(8,128)(2,1)S(1)} %bitcast.56), channel_id=1, source_target_pairs={{0,3},{1,0},{2,1},{3,2},{4,7},{5,4},{6,5},{7,6},{8,11},{9,8},{10,9... | collective-permute-start | bytes 638984 | tf_op jit(solution)/shard_map/ppermute | solution.py:36
  47.7 2.2 all-to-all-done.3
  49.9 3.0 %collective-permute-start.9 = (bf16[1,4,104,128]{3,2,0,1:T(8,128)(2,1)S(1)}, bf16[1,4,104,128]{3,2,0,1:T(8,128)(2,1)S(1)}, u32[]{:S(2)}, u32[]{:S(2)}) collective-permute-start(bf16[1,4,104,128]{3,2,0,1:T(8,128)(2,1)S(1)} %slice.212), channel_id=1, source_target_pairs={{0,32},{32,0},{1,33},{33,1},{2,34},{34,2},{3,35},{35,3},{4,36},{36... | collective-permute-start | bytes 319496 | tf_op jit(solution)/shard_map/ppermute | solution.py:27
  54.2 2.5 %collective-permute-start.15 = (bf16[2,1248,128]{2,1,0:T(8,128)(2,1)S(1)}, bf16[2,1248,128]{2,1,0:T(8,128)(2,1)S(1)}, u32[]{:S(2)}, u32[]{:S(2)}) collective-permute-start(bf16[2,1248,128]{2,1,0:T(8,128)(2,1)S(1)} %pad_maximum_fusion.1.refs_5_), channel_id=1, source_target_pairs={{0,3},{1,0},{2,1},{3,2},{4,7},{5,4},{6,5},{7,6},{8,11},{9,8},{10,9... | collective-permute-start | bytes 1916936 | tf_op jit(solution)/shard_map/ppermute | solution.py:36
  58.2 7.0 %collective-permute-done.11.refs_2_ = bf16[2,832,128]{2,1,0:T(8,128)(2,1)S(1)} collective-permute-done((bf16[2,832,128]{2,1,0:T(8,128)(2,1)S(1)}, bf16[2,832,128]{2,1,0:T(8,128)(2,1)S(1)}, u32[]{:S(2)}, u32[]{:S(2)}) %collective-permute-start.11) | collective-permute-done | bytes 426016 | tf_op jit(solution)/shard_map/ppermute | solution.py:36
  66.0 2.7 %collective-permute-done.10.refs_1_ = bf16[2,832,128]{2,1,0:T(8,128)(2,1)S(1)} collective-permute-done((bf16[2,832,128]{2,1,0:T(8,128)(2,1)S(1)}, bf16[2,832,128]{2,1,0:T(8,128)(2,1)S(1)}, u32[]{:S(2)}, u32[]{:S(2)}) %collective-permute-start.10) | collective-permute-done | bytes 426016 | tf_op jit(solution)/shard_map/ppermute | solution.py:36
  70.1 3.4 %collective-permute-start.3 = (bf16[416,128]{1,0:T(8,128)(2,1)S(1)}, bf16[416,128]{1,0:T(8,128)(2,1)S(1)}, u32[]{:S(2)}, u32[]{:S(2)}) collective-permute-start(bf16[416,128]{1,0:T(8,128)(2,1)S(1)} %slice_bitcast_fusion.8), channel_id=1, source_target_pairs={{0,3},{1,0},{2,1},{3,2},{4,7},{5,4},{6,5},{7,6},{8,11},{9,8},{10,9... | collective-permute-start | bytes 319496 | tf_op jit(solution)/shard_map/ppermute | solution.py:36
  74.3 9.3 %collective-permute-done.14.refs_6_ = bf16[2,1248,128]{2,1,0:T(8,128)(2,1)S(1)} collective-permute-done((bf16[2,1248,128]{2,1,0:T(8,128)(2,1)S(1)}, bf16[2,1248,128]{2,1,0:T(8,128)(2,1)S(1)}, u32[]{:S(2)}, u32[]{:S(2)}) %collective-permute-start.14) | collective-permute-done | bytes 639008 | tf_op jit(solution)/shard_map/ppermute | solution.py:36
  85.8 2.7 %collective-permute-start.17 = (bf16[1248,128]{1,0:T(8,128)(2,1)}, bf16[1248,128]{1,0:T(8,128)(2,1)}, u32[]{:S(2)}, u32[]{:S(2)}) collective-permute-start(bf16[1248,128]{1,0:T(8,128)(2,1)} %slice_bitcast_fusion), channel_id=1, source_target_pairs={{0,3},{1,0},{2,1},{3,2},{4,7},{5,4},{6,5},{7,6},{8,11},{9,8},{10,9... | collective-permute-start | bytes 958472 | tf_op jit(solution)/shard_map/ppermute | solution.py:36
  89.5 17.6 %shard_map.65 = bf16[16,1,224,128]{3,2,1,0:T(8,128)(2,1)} custom-call(bf16[2,416,128]{2,1,0:T(8,128)(2,1)S(1)} %bitcast.58, bf16[2,416,128]{2,1,0:T(8,128)(2,1)S(1)} %copy-done.9, bf16[2,416,128]{2,1,0:T(8,128)(2,1)S(1)} %copy-done.7, bf16[416,128]{1,0:T(8,128)(2,1)S(1)} %collective-permute-done.2.refs_3_, ...), custom_call_target="tpu_custom_call" | custom-call | flops 11341398016 | bytes 4194304 | tf_op jit(solution)/shard_map/pallas_call | solution.py:148
  107.1 8.7 %all-to-all-start.1 = ((bf16[16,1,224,128]{3,2,1,0:T(8,128)(2,1)}), bf16[16,1,224,128]{3,2,1,0:T(8,128)(2,1)}, u32[]{:S(2)}, u32[]{:S(2)}) async-start(bf16[16,1,224,128]{3,2,1,0:T(8,128)(2,1)} %shard_map.65), calls=%async_computation.1 | async-start | bytes 1835008 | tf_op jit(solution)/shard_map/all_to_all | solution.py:31
  117.8 27.8 %shard_map.67 = bf16[16,2,224,128]{3,2,1,0:T(8,128)(2,1)} custom-call(bf16[2,832,128]{2,1,0:T(8,128)(2,1)S(1)} %pad_maximum_fusion.2.refs_0_, bf16[2,832,128]{2,1,0:T(8,128)(2,1)S(1)} %copy-done.5, bf16[2,832,128]{2,1,0:T(8,128)(2,1)S(1)} %copy-done.3, bf16[832,128]{1,0:T(8,128)(2,1)} %collective-permute-done.12.refs_3_, ...), custom_call_target="tpu_custom_call" | custom-call | flops 17012097024 | bytes 4194304 | tf_op jit(solution)/shard_map/pallas_call | solution.py:148
  145.7 4.3 %all-to-all-start.4 = ((bf16[16,2,224,128]{3,2,1,0:T(8,128)(2,1)}), bf16[16,2,224,128]{3,2,1,0:T(8,128)(2,1)}, u32[]{:S(2)}, u32[]{:S(2)}) async-start(bf16[16,2,224,128]{3,2,1,0:T(8,128)(2,1)} %shard_map.67), calls=%async_computation.4 | async-start | bytes 3670016 | tf_op jit(solution)/shard_map/all_to_all | solution.py:31
  150.0 2.3 %shard_map.66 = bf16[2,208,256]{2,1,0:T(8,128)(2,1)} custom-call(bf16[16,1,224,128]{3,2,1,0:T(8,128)(2,1)} %all-to-all-done.1.x), custom_call_target="tpu_custom_call" | custom-call | tf_op jit(solution)/shard_map/pallas_call | solution.py:195
  154.2 3.2 %fusion.8 = f32[208,2560]{1,0:T(8,128)} fusion(bf16[640,5120]{1,0:T(8,128)(2,1)} %param.10, pred[]{:T(512)S(6)} %eq.5, bf16[2,208,256]{2,1,0:T(8,128)(2,1)S(1)} %copy-done.11), kind=kOutput, calls=%fused_computation.14 | convolution fusion | flops 272683008 | bytes 3653633 | tf_op jit(solution)/shard_map/dot_general | solution.py:250
  157.4 21.7 %all-to-all-done.4.x = bf16[16,2,224,128]{3,2,1,0:T(8,128)(2,1)} async-done(((bf16[16,2,224,128]{3,2,1,0:T(8,128)(2,1)}), bf16[16,2,224,128]{3,2,1,0:T(8,128)(2,1)}, u32[]{:S(2)}, u32[]{:S(2)}) %all-to-all-start.4) | async-done | bytes 1835040 | tf_op jit(solution)/shard_map/all_to_all | solution.py:31
  179.1 3.0 %shard_map.68 = bf16[2,208,384]{2,1,0:T(8,128)(2,1)} custom-call(bf16[16,2,224,128]{3,2,1,0:T(8,128)(2,1)} %all-to-all-done.4.x), custom_call_target="tpu_custom_call" | custom-call | tf_op jit(solution)/shard_map/pallas_call | solution.py:195
  182.1 2.5 %convolution_add_fusion.5 = f32[208,2560]{1,0:T(8,128)S(1)} fusion(f32[208,2560]{1,0:T(8,128)} %fusion.8, bf16[640,5120]{1,0:T(8,128)(2,1)} %collective-permute-done.8, pred[]{:T(512)S(6)} %eq.5, bf16[2,208,256]{2,1,0:T(8,128)(2,1)S(1)} %copy-done.11), kind=kOutput, calls=%fused_computation.5 | convolution fusion | flops 273215488 | bytes 5783553 | tf_op jit(solution)/shard_map/dot_general | solution.py:250
  184.7 2.3 %convolution_add_fusion.4 = f32[208,2560]{1,0:T(8,128)S(1)} fusion(f32[208,2560]{1,0:T(8,128)S(1)} %convolution_add_fusion.5, bf16[640,5120]{1,0:T(8,128)(2,1)} %param.10, pred[]{:T(512)S(6)} %eq.5, bf16[2,208,384]{2,1,0:T(8,128)(2,1)S(1)} %copy-done.10), kind=kOutput, calls=%fused_computation.4 | convolution fusion | flops 409556992 | bytes 6545409 | tf_op jit(solution)/shard_map/dot_general | solution.py:250
  188.7 2.3 %convolution_add_fusion.1 = f32[208,2560]{1,0:T(8,128)S(1)} fusion(f32[208,2560]{1,0:T(8,128)S(1)} %convolution_add_fusion.2, bf16[640,5120]{1,0:T(8,128)(2,1)} %param.10, pred[]{:T(512)S(6)} %eq.5, bf16[2,208,384]{2,1,0:T(8,128)(2,1)S(1)} %copy-done.10), kind=kOutput, calls=%fused_computation.1 | convolution fusion | flops 409556992 | bytes 6545409 | tf_op jit(solution)/shard_map/dot_general | solution.py:250
  191.0 2.3 %convolution_add_fusion = f32[208,2560]{1,0:T(8,128)S(1)} fusion(f32[208,2560]{1,0:T(8,128)S(1)} %convolution_add_fusion.1, bf16[640,5120]{1,0:T(8,128)(2,1)} %collective-permute-done.8, pred[]{:T(512)S(6)} %eq.5, bf16[2,208,384]{2,1,0:T(8,128)(2,1)S(1)} %copy-done.10), kind=kOutput, calls=%fused_computation | convolution fusion | flops 409556992 | bytes 6545409 | tf_op jit(solution)/shard_map/dot_general | solution.py:250
  193.4 2.3 %convolution_add_fusion.3 = f32[208,2560]{1,0:T(8,128)S(1)} fusion(f32[208,2560]{1,0:T(8,128)S(1)} %convolution_add_fusion.4, bf16[640,5120]{1,0:T(8,128)(2,1)} %collective-permute-done.8, pred[]{:T(512)S(6)} %eq.5, bf16[2,208,384]{2,1,0:T(8,128)(2,1)S(1)} %copy-done.10), kind=kOutput, calls=%fused_computation.3 | convolution fusion | flops 409556992 | bytes 6545409 | tf_op jit(solution)/shard_map/dot_general | solution.py:250
  198.6 12.7 %collective-permute-done.18 = bf16[104,2560]{1,0:T(8,128)(2,1)S(1)} collective-permute-done((bf16[104,2560]{1,0:T(8,128)(2,1)S(1)}, bf16[104,2560]{1,0:T(8,128)(2,1)S(1)}, u32[]{:S(2)}, u32[]{:S(2)}) %collective-permute-start.18) | collective-permute-done | bytes 532512 | tf_op jit(solution)/shard_map/ppermute | solution.py:27
  211.3 9.2 %collective-permute-done.19 = bf16[104,2560]{1,0:T(8,128)(2,1)S(1)} collective-permute-done((bf16[104,2560]{1,0:T(8,128)(2,1)S(1)}, bf16[104,2560]{1,0:T(8,128)(2,1)S(1)}, u32[]{:S(2)}, u32[]{:S(2)}) %collective-permute-start.19) | collective-permute-done | bytes 532512 | tf_op jit(solution)/shard_map/ppermute | solution.py:27
  (97 shorter events, 21.2 us)
Async XLA Ops:
  2.8 17.4 %all-to-all-start = ((bf16[8,3,104,128]{3,2,1,0:T(8,128)(2,1)}), bf16[8,3,104,128]{3,2,1,0:T(8,128)(2,1)S(1)}, u32[]{:S(2)}, u32[]{:S(2)}) async-start(bf16[8,3,104,128]{3,2,1,0:T(8,128)(2,1)} %get-tuple-element.15), calls=%async_computation | async-start | bytes 1277952 | tf_op jit(solution)/shard_map/all_to_all | solution.py:31
  9.6 172.5 %collective-permute-start.8 = (bf16[640,5120]{1,0:T(8,128)(2,1)}, bf16[640,5120]{1,0:T(8,128)(2,1)}, u32[]{:S(2)}, u32[]{:S(2)}) collective-permute-start(bf16[640,5120]{1,0:T(8,128)(2,1)} %param.10), channel_id=1, source_target_pairs={{0,32},{32,0},{1,33},{33,1},{2,34},{34,2},{3,35},{35,3},{4,36},{36... | collective-permute-start | bytes 19660808 | tf_op jit(solution)/shard_map/ppermute | solution.py:27
  20.2 20.0 %all-to-all-start.2 = ((bf16[8,3,104,128]{3,2,1,0:T(8,128)(2,1)}), bf16[8,3,104,128]{3,2,1,0:T(8,128)(2,1)S(1)}, u32[]{:S(2)}, u32[]{:S(2)}) async-start(bf16[8,3,104,128]{3,2,1,0:T(8,128)(2,1)} %get-tuple-element.18), calls=%async_computation.2 | async-start | bytes 1277952 | tf_op jit(solution)/shard_map/all_to_all | solution.py:31
  24.1 12.0 %collective-permute-start.5 = (bf16[2,832,128]{2,1,0:T(8,128)(2,1)S(1)}, bf16[2,832,128]{2,1,0:T(8,128)(2,1)S(1)}, u32[]{:S(2)}, u32[]{:S(2)}) collective-permute-start(bf16[2,832,128]{2,1,0:T(8,128)(2,1)S(1)} %bitcast.53), channel_id=1, source_target_pairs={{0,24},{8,0},{16,8},{24,16},{1,25},{9,1},{17,9},{25,17},{2,26},{10... | collective-permute-start | bytes 1277960 | tf_op jit(solution)/shard_map/ppermute | solution.py:36
  27.0 19.8 %collective-permute-start.4 = (bf16[2,832,128]{2,1,0:T(8,128)(2,1)S(1)}, bf16[2,832,128]{2,1,0:T(8,128)(2,1)S(1)}, u32[]{:S(2)}, u32[]{:S(2)}) collective-permute-start(bf16[2,832,128]{2,1,0:T(8,128)(2,1)S(1)} %bitcast.54), channel_id=1, source_target_pairs={{0,8},{8,16},{16,24},{24,0},{1,9},{9,17},{17,25},{25,1},{2,10},{10... | collective-permute-start | bytes 1277960 | tf_op jit(solution)/shard_map/ppermute | solution.py:36
  36.8 47.5 %collective-permute-start.7 = (bf16[832,128]{1,0:T(8,128)(2,1)}, bf16[832,128]{1,0:T(8,128)(2,1)}, u32[]{:S(2)}, u32[]{:S(2)}) collective-permute-start(bf16[832,128]{1,0:T(8,128)(2,1)} %slice_bitcast_fusion.5), channel_id=1, source_target_pairs={{0,24},{8,0},{16,8},{24,16},{1,25},{9,1},{17,9},{25,17},{2,26},{10... | collective-permute-start | bytes 638984 | tf_op jit(solution)/shard_map/ppermute | solution.py:36
  40.2 9.7 %all-to-all-start.3 = ((bf16[4,3,104,128]{3,2,1,0:T(8,128)(2,1)}), bf16[4,3,104,128]{3,2,1,0:T(8,128)(2,1)S(1)}, u32[]{:S(2)}, u32[]{:S(2)}) async-start(bf16[4,3,104,128]{3,2,1,0:T(8,128)(2,1)} %get-tuple-element.20), calls=%async_computation.3 | async-start | bytes 638976 | tf_op jit(solution)/shard_map/all_to_all | solution.py:31
  44.2 8.7 %collective-permute-start.1 = (bf16[2,416,128]{2,1,0:T(8,128)(2,1)S(1)}, bf16[2,416,128]{2,1,0:T(8,128)(2,1)S(1)}, u32[]{:S(2)}, u32[]{:S(2)}) collective-permute-start(bf16[2,416,128]{2,1,0:T(8,128)(2,1)S(1)} %bitcast.56), channel_id=1, source_target_pairs={{0,3},{1,0},{2,1},{3,2},{4,7},{5,4},{6,5},{7,6},{8,11},{9,8},{10,9... | collective-permute-start | bytes 638984 | tf_op jit(solution)/shard_map/ppermute | solution.py:36
  46.8 6.2 %copy-start = (bf16[2,832,128]{2,1,0:T(8,128)(2,1)}, bf16[2,832,128]{2,1,0:T(8,128)(2,1)S(1)}, u32[]{:S(2)}) copy-start(bf16[2,832,128]{2,1,0:T(8,128)(2,1)S(1)} %collective-permute-done.4.refs_6_) | copy-start | bytes 1277956
  47.6 9.2 %collective-permute-start = (bf16[2,416,128]{2,1,0:T(8,128)(2,1)S(1)}, bf16[2,416,128]{2,1,0:T(8,128)(2,1)S(1)}, u32[]{:S(2)}, u32[]{:S(2)}) collective-permute-start(bf16[2,416,128]{2,1,0:T(8,128)(2,1)S(1)} %bitcast.57), channel_id=1, source_target_pairs={{0,1},{1,2},{2,3},{3,0},{4,5},{5,6},{6,7},{7,4},{8,9},{9,10},{10,1... | collective-permute-start | bytes 638984 | tf_op jit(solution)/shard_map/ppermute | solution.py:36
  49.9 3.9 %collective-permute-start.9 = (bf16[1,4,104,128]{3,2,0,1:T(8,128)(2,1)S(1)}, bf16[1,4,104,128]{3,2,0,1:T(8,128)(2,1)S(1)}, u32[]{:S(2)}, u32[]{:S(2)}) collective-permute-start(bf16[1,4,104,128]{3,2,0,1:T(8,128)(2,1)S(1)} %slice.212), channel_id=1, source_target_pairs={{0,32},{32,0},{1,33},{33,1},{2,34},{34,2},{3,35},{35,3},{4,36},{36... | collective-permute-start | bytes 319496 | tf_op jit(solution)/shard_map/ppermute | solution.py:27
  53.0 12.2 %copy-start.13 = (bf16[832,128]{1,0:T(8,128)(2,1)S(1)}, bf16[832,128]{1,0:T(8,128)(2,1)}, u32[]{:S(2)}) copy-start(bf16[832,128]{1,0:T(8,128)(2,1)} %slice_bitcast_fusion.6) | copy-start | bytes 638980
  54.0 34.5 %copy-start.1 = (bf16[2,832,128]{2,1,0:T(8,128)(2,1)S(1)}, bf16[2,832,128]{2,1,0:T(8,128)(2,1)}, u32[]{:S(2)}) copy-start(bf16[2,832,128]{2,1,0:T(8,128)(2,1)} %copy-done) | copy-start | bytes 1277956
  54.0 11.1 %collective-permute-start.11 = (bf16[2,832,128]{2,1,0:T(8,128)(2,1)S(1)}, bf16[2,832,128]{2,1,0:T(8,128)(2,1)S(1)}, u32[]{:S(2)}, u32[]{:S(2)}) collective-permute-start(bf16[2,832,128]{2,1,0:T(8,128)(2,1)S(1)} %pad_maximum_fusion.2.refs_0_), channel_id=1, source_target_pairs={{0,24},{8,0},{16,8},{24,16},{1,25},{9,1},{17,9},{25,17},{2,26},{10... | collective-permute-start | bytes 1277960 | tf_op jit(solution)/shard_map/ppermute | solution.py:36
  54.1 34.4 %copy-start.7 = (bf16[2,416,128]{2,1,0:T(8,128)(2,1)S(1)}, bf16[2,416,128]{2,1,0:T(8,128)(2,1)}, u32[]{:S(2)}) copy-start(bf16[2,416,128]{2,1,0:T(8,128)(2,1)} %copy-done.6) | copy-start | bytes 638980
  54.2 16.0 %collective-permute-start.15 = (bf16[2,1248,128]{2,1,0:T(8,128)(2,1)S(1)}, bf16[2,1248,128]{2,1,0:T(8,128)(2,1)S(1)}, u32[]{:S(2)}, u32[]{:S(2)}) collective-permute-start(bf16[2,1248,128]{2,1,0:T(8,128)(2,1)S(1)} %pad_maximum_fusion.1.refs_5_), channel_id=1, source_target_pairs={{0,3},{1,0},{2,1},{3,2},{4,7},{5,4},{6,5},{7,6},{8,11},{9,8},{10,9... | collective-permute-start | bytes 1916936 | tf_op jit(solution)/shard_map/ppermute | solution.py:36
  56.7 9.2 %copy-start.8 = (bf16[2,416,128]{2,1,0:T(8,128)(2,1)}, bf16[2,416,128]{2,1,0:T(8,128)(2,1)S(1)}, u32[]{:S(2)}) copy-start(bf16[2,416,128]{2,1,0:T(8,128)(2,1)S(1)} %collective-permute-done.refs_1_) | copy-start | bytes 638980
  56.7 11.9 %collective-permute-start.10 = (bf16[2,832,128]{2,1,0:T(8,128)(2,1)S(1)}, bf16[2,832,128]{2,1,0:T(8,128)(2,1)S(1)}, u32[]{:S(2)}, u32[]{:S(2)}) collective-permute-start(bf16[2,832,128]{2,1,0:T(8,128)(2,1)S(1)} %pad_maximum_fusion.2.refs_0_), channel_id=1, source_target_pairs={{0,8},{8,16},{16,24},{24,0},{1,9},{9,17},{17,25},{25,1},{2,10},{10... | collective-permute-start | bytes 1277960 | tf_op jit(solution)/shard_map/ppermute | solution.py:36
  65.1 19.8 %collective-permute-start.6 = (bf16[832,128]{1,0:T(8,128)(2,1)S(1)}, bf16[832,128]{1,0:T(8,128)(2,1)S(1)}, u32[]{:S(2)}, u32[]{:S(2)}) collective-permute-start(bf16[832,128]{1,0:T(8,128)(2,1)S(1)} %copy-done.13), channel_id=1, source_target_pairs={{0,8},{8,16},{16,24},{24,0},{1,9},{9,17},{17,25},{25,1},{2,10},{10... | collective-permute-start | bytes 638984 | tf_op jit(solution)/shard_map/ppermute | solution.py:36
  68.7 14.9 %copy-start.4 = (bf16[2,832,128]{2,1,0:T(8,128)(2,1)}, bf16[2,832,128]{2,1,0:T(8,128)(2,1)S(1)}, u32[]{:S(2)}) copy-start(bf16[2,832,128]{2,1,0:T(8,128)(2,1)S(1)} %collective-permute-done.10.refs_1_) | copy-start | bytes 1277956
  68.7 14.9 %collective-permute-start.14 = (bf16[2,1248,128]{2,1,0:T(8,128)(2,1)S(1)}, bf16[2,1248,128]{2,1,0:T(8,128)(2,1)S(1)}, u32[]{:S(2)}, u32[]{:S(2)}) collective-permute-start(bf16[2,1248,128]{2,1,0:T(8,128)(2,1)S(1)} %pad_maximum_fusion.1.refs_5_), channel_id=1, source_target_pairs={{0,1},{1,2},{2,3},{3,0},{4,5},{5,6},{6,7},{7,4},{8,9},{9,10},{10,1... | collective-permute-start | bytes 1916936 | tf_op jit(solution)/shard_map/ppermute | solution.py:36
  70.1 15.7 %collective-permute-start.3 = (bf16[416,128]{1,0:T(8,128)(2,1)S(1)}, bf16[416,128]{1,0:T(8,128)(2,1)S(1)}, u32[]{:S(2)}, u32[]{:S(2)}) collective-permute-start(bf16[416,128]{1,0:T(8,128)(2,1)S(1)} %slice_bitcast_fusion.8), channel_id=1, source_target_pairs={{0,3},{1,0},{2,1},{3,2},{4,7},{5,4},{6,5},{7,6},{8,11},{9,8},{10,9... | collective-permute-start | bytes 319496 | tf_op jit(solution)/shard_map/ppermute | solution.py:36
  83.6 4.9 %collective-permute-start.2 = (bf16[416,128]{1,0:T(8,128)(2,1)S(1)}, bf16[416,128]{1,0:T(8,128)(2,1)S(1)}, u32[]{:S(2)}, u32[]{:S(2)}) collective-permute-start(bf16[416,128]{1,0:T(8,128)(2,1)S(1)} %slice_bitcast_fusion.9), channel_id=1, source_target_pairs={{0,1},{1,2},{2,3},{3,0},{4,5},{5,6},{6,7},{7,4},{8,9},{9,10},{10,1... | collective-permute-start | bytes 319496 | tf_op jit(solution)/shard_map/ppermute | solution.py:36
  84.3 31.4 %collective-permute-start.13 = (bf16[832,128]{1,0:T(8,128)(2,1)}, bf16[832,128]{1,0:T(8,128)(2,1)}, u32[]{:S(2)}, u32[]{:S(2)}) collective-permute-start(bf16[832,128]{1,0:T(8,128)(2,1)} %slice_bitcast_fusion.2), channel_id=1, source_target_pairs={{0,24},{8,0},{16,8},{24,16},{1,25},{9,1},{17,9},{25,17},{2,26},{10... | collective-permute-start | bytes 638984 | tf_op jit(solution)/shard_map/ppermute | solution.py:36
  85.0 30.8 %collective-permute-start.12 = (bf16[832,128]{1,0:T(8,128)(2,1)}, bf16[832,128]{1,0:T(8,128)(2,1)}, u32[]{:S(2)}, u32[]{:S(2)}) collective-permute-start(bf16[832,128]{1,0:T(8,128)(2,1)} %slice_bitcast_fusion.3), channel_id=1, source_target_pairs={{0,8},{8,16},{16,24},{24,0},{1,9},{9,17},{17,25},{25,1},{2,10},{10... | collective-permute-start | bytes 638984 | tf_op jit(solution)/shard_map/ppermute | solution.py:36
  85.8 30.0 %collective-permute-start.17 = (bf16[1248,128]{1,0:T(8,128)(2,1)}, bf16[1248,128]{1,0:T(8,128)(2,1)}, u32[]{:S(2)}, u32[]{:S(2)}) collective-permute-start(bf16[1248,128]{1,0:T(8,128)(2,1)} %slice_bitcast_fusion), channel_id=1, source_target_pairs={{0,3},{1,0},{2,1},{3,2},{4,7},{5,4},{6,5},{7,6},{8,11},{9,8},{10,9... | collective-permute-start | bytes 958472 | tf_op jit(solution)/shard_map/ppermute | solution.py:36
  88.5 27.3 %collective-permute-start.16 = (bf16[1248,128]{1,0:T(8,128)(2,1)}, bf16[1248,128]{1,0:T(8,128)(2,1)}, u32[]{:S(2)}, u32[]{:S(2)}) collective-permute-start(bf16[1248,128]{1,0:T(8,128)(2,1)} %slice_bitcast_fusion.1), channel_id=1, source_target_pairs={{0,1},{1,2},{2,3},{3,0},{4,5},{5,6},{6,7},{7,4},{8,9},{9,10},{10,1... | collective-permute-start | bytes 958472 | tf_op jit(solution)/shard_map/ppermute | solution.py:36
  107.1 38.6 %all-to-all-start.1 = ((bf16[16,1,224,128]{3,2,1,0:T(8,128)(2,1)}), bf16[16,1,224,128]{3,2,1,0:T(8,128)(2,1)}, u32[]{:S(2)}, u32[]{:S(2)}) async-start(bf16[16,1,224,128]{3,2,1,0:T(8,128)(2,1)} %shard_map.65), calls=%async_computation.1 | async-start | bytes 1835008 | tf_op jit(solution)/shard_map/all_to_all | solution.py:31
  145.7 33.5 %all-to-all-start.4 = ((bf16[16,2,224,128]{3,2,1,0:T(8,128)(2,1)}), bf16[16,2,224,128]{3,2,1,0:T(8,128)(2,1)}, u32[]{:S(2)}, u32[]{:S(2)}) async-start(bf16[16,2,224,128]{3,2,1,0:T(8,128)(2,1)} %shard_map.67), calls=%async_computation.4 | async-start | bytes 3670016 | tf_op jit(solution)/shard_map/all_to_all | solution.py:31
  195.7 24.8 %copy-start.12 = (bf16[104,5120]{1,0:T(8,128)(2,1)S(1)}, bf16[104,5120]{1,0:T(8,128)(2,1)}, u32[]{:S(2)}) copy-start(bf16[104,5120]{1,0:T(8,128)(2,1)} %param.9) | copy-start | bytes 3194884
  195.9 15.5 %collective-permute-start.18 = (bf16[104,2560]{1,0:T(8,128)(2,1)S(1)}, bf16[104,2560]{1,0:T(8,128)(2,1)S(1)}, u32[]{:S(2)}, u32[]{:S(2)}) collective-permute-start(bf16[104,2560]{1,0:T(8,128)(2,1)S(1)} %select_convert_fusion.1), channel_id=1, source_target_pairs={{0,68},{4,64},{64,4},{68,0},{1,69},{5,65},{65,5},{69,1},{2,70},{6,... | collective-permute-start | bytes 1597448 | tf_op jit(solution)/shard_map/ppermute | solution.py:27
  196.8 23.8 %collective-permute-start.19 = (bf16[104,2560]{1,0:T(8,128)(2,1)S(1)}, bf16[104,2560]{1,0:T(8,128)(2,1)S(1)}, u32[]{:S(2)}, u32[]{:S(2)}) collective-permute-start(bf16[104,2560]{1,0:T(8,128)(2,1)S(1)} %select_convert_fusion), channel_id=1, source_target_pairs={{0,68},{4,64},{64,4},{68,0},{1,69},{5,65},{65,5},{69,1},{2,70},{6,... | collective-permute-start | bytes 1597448 | tf_op jit(solution)/shard_map/ppermute | solution.py:27
  (8 other events, 14.7 us)
